TPU v7x, 32 devices: a whole 2x2x4 slice. The times are simulated.
32 devices in a mesh: dp: 8 (over z, x), mp: 4 (over y, core).
Axes of the slice: x: 2, y: 2, z: 4, core: 2. Of those that a mesh axis runs over, the one named last changes fastest.
Arguments:
- teacher_in: bfloat16 [512, 16384], P('dp', 'mp'), may hold values from -6 to 6
- teacher_weight: bfloat16 [16384, 8192], P('mp', 'dp'), may hold values from -0.046875 to 0.046875
- student_in: bfloat16 [512, 8192], P('dp', 'mp'), may hold values from -6 to 6
- projection: bfloat16 [8192, 8192], P('mp', 'dp'), may hold values from -0.0625 to 0.0625
- owner_order: int32 [512], P('mp'), may hold values from 0 to 127, as said below
Outputs:
- projection_grad: float32 [8192, 8192], P('mp', 'dp')
- cosine: float32 [512], P('mp')
Inputs may be any that keep to these rules, and one draw needn't show every extreme that they name: `owner_order`: each aligned block of 128 entries is a permutation of 0 to 127.
All inputs are finite; a program needn't handle non-finite values.
Results may differ from a plain program's by a relative error of at most 0.025.
Values may be sent and summed in bfloat16 or wider, within the bound.
A program may use at most 64 MiB of HBM per device.

v0:
```python
import jax
import jax.numpy as jnp
from jax import lax
from jax.sharding import PartitionSpec as P


def shards(teacher_in, teacher_weight, student_in, projection, owner_order):
    teacher_all = lax.all_gather(teacher_in, "dp", axis=0, tiled=True)
    student_all = lax.all_gather(student_in, "dp", axis=0, tiled=True)
    groups = lax.axis_size("mp")
    total_rows = teacher_all.shape[0]
    block_len = total_rows // groups
    sub_len = block_len // groups
    slab = teacher_all
    owned = lax.psum_scatter(
        jnp.dot(slab, teacher_weight, preferred_element_type=jnp.float32).astype(jnp.bfloat16),
        "mp",
        scatter_dimension=0,
        tiled=True,
    )
    picked = owned[owner_order].reshape(groups, sub_len, owned.shape[1])
    arrived = lax.all_to_all(picked, "mp", split_axis=0, concat_axis=0, tiled=True)
    target = arrived.reshape(block_len, owned.shape[1])
    slab = student_all
    student_out = lax.psum_scatter(
        jnp.dot(slab, projection, preferred_element_type=jnp.float32).astype(jnp.bfloat16),
        "mp",
        scatter_dimension=0,
        tiled=True,
    ).astype(jnp.float32)
    target_f = target.astype(jnp.float32)
    inner, sq_student, sq_target = lax.psum(
        (
            jnp.sum(student_out * target_f, axis=1),
            jnp.sum(student_out * student_out, axis=1),
            jnp.sum(target_f * target_f, axis=1),
        ),
        "dp",
    )
    inv_student = lax.rsqrt(sq_student + 1e-06)
    inv_target = lax.rsqrt(sq_target + 1e-06)
    cosine = inner * inv_student * inv_target
    scale = -1.0 / total_rows
    grad_out = scale * (
        target_f * (inv_student * inv_target)[:, None]
        - (inner * inv_target * inv_student**3)[:, None] * student_out
    )
    grad_out = grad_out.astype(jnp.bfloat16)
    projection_grad = lax.dot_general(
        student_all,
        lax.all_gather(grad_out, "mp", axis=0, tiled=True),
        (((0,), (0,)), ((), ())),
        preferred_element_type=jnp.float32,
    )
    return (projection_grad, cosine)


def solution(mesh):
    return jax.shard_map(
        shards,
        mesh=mesh,
        in_specs=(P("dp", "mp"), P("mp", "dp"), P("dp", "mp"), P("mp", "dp"), P("mp")),
        out_specs=(P("mp", "dp"), P("mp")),
        check_vma=False,
    )
```

profile of v0, /device:TPU:0, one launch (start us, length us, event | category | flops | bytes accessed | tf_op | source)
XLA Modules:
  0.0 250.6 jit_solution(16635514056273890234)
XLA Ops:
  7.2 0.0 all-gather.4.cloned.1.call-start
  7.2 0.7 all-gather.4.cloned.1.call-update
  7.9 0.0 all-gather.6.cloned.1.call-start
  7.9 0.7 all-gather.6.cloned.1.call-update
  8.6 0.0 reduce-scatter.3.cloned.1.call-start
  8.7 77.6 %all-gather.4.cloned.1.call-done = bf16[512,4096]{1,0:T(8,128)(2,1)} async-done(((bf16[64,4096]{1,0:T(8,128)(2,1)}), bf16[512,4096]{1,0:T(8,128)(2,1)}) %all-gather.4.cloned.1.call-update) | async-done | bytes 4194320 | tf_op jit(solution)/shard_map/all_gather | solution.py:8
  86.3 10.1 %convolution_convert_fusion = bf16[512,1024]{1,0:T(8,128)(2,1)} fusion(bf16[512,4096]{1,0:T(8,128)(2,1)} %all-gather.4.cloned.1.call-done, bf16[4096,1024]{1,0:T(8,128)(2,1)} %param.6), kind=kOutput, calls=%fused_computation.2 | convolution fusion | flops 4295491584 | bytes 13631488 | tf_op jit(solution)/shard_map/dot_general | solution.py:16
  96.4 0.0 reduce-scatter.3.cloned.1.call-update
  96.4 0.0 copy-start.1
  96.4 0.0 reduce-scatter.5.cloned.1.call-start
  96.5 39.5 %all-gather.6.cloned.1.call-done = bf16[512,2048]{1,0:T(8,128)(2,1)} async-done(((bf16[64,2048]{1,0:T(8,128)(2,1)}), bf16[512,2048]{1,0:T(8,128)(2,1)}) %all-gather.6.cloned.1.call-update) | async-done | bytes 2097168 | tf_op jit(solution)/shard_map/all_gather | solution.py:9
  136.0 6.1 %convolution_convert_fusion.1 = bf16[512,1024]{1,0:T(8,128)(2,1)} fusion(bf16[512,2048]{1,0:T(8,128)(2,1)} %all-gather.6.cloned.1.call-done, bf16[2048,1024]{1,0:T(8,128)(2,1)} %param.8), kind=kOutput, calls=%fused_computation.3 | convolution fusion | flops 2148007936 | bytes 7340032 | tf_op jit(solution)/shard_map/dot_general | solution.py:26
  142.1 0.0 copy-start
  142.1 0.0 reduce-scatter.5.cloned.1.call-update
  142.1 0.0 all-gather.8.cloned.1.call-start
  142.2 0.0 copy-done.1
  142.2 19.7 %reduce-scatter.3.cloned.1.call-done = bf16[128,1024]{1,0:T(8,128)(2,1)} async-done(((bf16[512,1024]{1,0:T(8,128)(2,1)}), bf16[128,1024]{1,0:T(8,128)(2,1)}) %reduce-scatter.3.cloned.1.call-update) | async-done | bytes 262160 | tf_op jit(solution)/shard_map/reduce_scatter | solution.py:15
  161.9 2.0 gather_fusion
  163.9 8.4 %all_to_all.5 = bf16[4,32,1024]{2,1,0:T(8,128)(2,1)S(1)} all-to-all(bf16[4,32,1024]{2,1,0:T(8,128)(2,1)S(1)} %bitcast.14), channel_id=1, replica_groups=mesh['dp'=8,'mp'=4] {'mp'}, dimensions={0} | all-to-all | bytes 524288 | tf_op jit(solution)/shard_map/all_to_all | solution.py:22
  172.4 0.1 fusion.5
  172.5 0.1 reduce_sum.31
  172.6 17.4 %reduce-scatter.5.cloned.1.call-done = bf16[128,1024]{1,0:T(8,128)(2,1)} async-done(((bf16[512,1024]{1,0:T(8,128)(2,1)}), bf16[128,1024]{1,0:T(8,128)(2,1)}) %reduce-scatter.5.cloned.1.call-update) | async-done | bytes 262160 | tf_op jit(solution)/shard_map/reduce_scatter | solution.py:25
  189.9 1.1 fusion
  191.1 21.4 %all-reduce = (f32[128]{0:T(128)S(1)}, f32[128]{0:T(128)S(1)}, f32[128]{0:T(128)S(1)}) all-reduce(f32[128]{0:T(128)S(1)} %get-tuple-element.5, f32[128]{0:T(128)S(1)} %get-tuple-element.4, f32[128]{0:T(128)S(1)} %reduce_sum.31), channel_id=1, replica_groups=mesh['dp'=8,'mp'=4] {'dp'}, use_global_device_ids=true, to_apply=%region_7.0 | all-reduce | flops 384 | bytes 3072 | tf_op jit(solution)/shard_map/psum | solution.py:32
  212.4 0.5 multiply_multiply_fusion.1
  213.0 1.8 fusion.4
  214.8 0.0 all-gather.8.cloned.1.call-update
  214.8 13.2 %all-gather.8.cloned.1.call-done = bf16[512,1024]{1,0:T(8,128)(2,1)} async-done(((bf16[128,1024]{1,0:T(8,128)(2,1)}), bf16[512,1024]{1,0:T(8,128)(2,1)}) %all-gather.8.cloned.1.call-update) | async-done | bytes 1048592 | tf_op jit(solution)/shard_map/all_gather | solution.py:51
  228.0 0.0 copy-done
  228.0 6.8 %convolution_bitcast_fusion = f32[2048,1024]{0,1:T(8,128)} fusion(bf16[512,1024]{1,0:T(8,128)(2,1)} %all-gather.8.cloned.1.call-done, bf16[512,2048]{1,0:T(8,128)(2,1)S(1)} %copy-done), kind=kOutput, calls=%fused_computation.1 | convolution fusion | flops 2147483648 | bytes 11534336 | tf_op jit(solution)/shard_map/dot_general | solution.py:49
  234.8 9.2 %copy.7 = f32[2048,1024]{1,0:T(8,128)} copy(f32[2048,1024]{0,1:T(8,128)} %convolution_bitcast_fusion) | data formatting | bytes 16777216
  (2 shorter events, 0.0 us)
Async XLA Ops:
  7.2 79.1 %all-gather.4.cloned.1.call-start = ((), (), s32[]{:S(2)}) async-start(), calls=%async_computation.3 | async-start | bytes 4718592 | tf_op jit(solution)/shard_map/all_gather | solution.py:8
  7.9 128.1 %all-gather.6.cloned.1.call-start = ((), (), s32[]{:S(2)}) async-start(), calls=%async_computation.5 | async-start | bytes 2359296 | tf_op jit(solution)/shard_map/all_gather | solution.py:9
  8.6 153.3 %reduce-scatter.3.cloned.1.call-start = ((), (), s32[]{:S(2)}) async-start(), calls=%async_computation.4 | async-start | bytes 1310720 | tf_op jit(solution)/shard_map/reduce_scatter | solution.py:15
  96.4 45.7 %copy-start.1 = (s32[128]{0:T(128)S(1)}, s32[128]{0:T(128)}, u32[]{:S(2)}) copy-start(s32[128]{0:T(128)} %param.9) | copy-start | bytes 1540
  96.4 93.5 %reduce-scatter.5.cloned.1.call-start = ((), (), s32[]{:S(2)}) async-start(), calls=%async_computation.6 | async-start | bytes 1310720 | tf_op jit(solution)/shard_map/reduce_scatter | solution.py:25
  142.1 85.9 %copy-start = (bf16[512,2048]{1,0:T(8,128)(2,1)S(1)}, bf16[512,2048]{1,0:T(8,128)(2,1)}, u32[]{:S(2)}) copy-start(bf16[512,2048]{1,0:T(8,128)(2,1)} %all-gather.6.cloned.1.call-done) | copy-start | bytes 6291460
  142.1 85.9 %all-gather.8.cloned.1.call-start = ((), (), s32[]{:S(2)}) async-start(), calls=%async_computation.7 | async-start | bytes 1310720 | tf_op jit(solution)/shard_map/all_gather | solution.py:51
Sparse Core Ops, SparseCore 0:
  10.1 76.0 all-gather.3
  88.4 47.5 all-gather.5
  138.5 23.3 reduce-scatter.2
  165.0 24.8 reduce-scatter.4
  214.9 13.0 all-gather.7
where the time goes:
time: 251 us
  waiting for transfers between devices  169 us (67%)
  blocking collectives  29.8 us (12%)
  matrix products  23.1 us (9%)
  between operations  13.8 us (5%)
  local copies, waits for them, and re-layouts  11.4 us (5%)
  other arithmetic  3.62 us (1%)
    all_gather x1, waiting for transfers between devices, shards(): teacher_all = lax.all_gather(teacher_in, 'dp', axis=0, tiled=True)  77.6 us
    all_gather x1, waiting for transfers between devices, shards(): student_all = lax.all_gather(student_in, 'dp', axis=0, tiled=True)  39.5 us
    psum x1, blocking collectives, shards(): lax.psum((jnp.sum(student_out * target_f, axis=1), jnp.sum(student_out *...  21.4 us
    reduce_scatter x1, waiting for transfers between devices, shards(): lax.psum_scatter(jnp.dot(slab, teacher_weight, preferred_element_type=jnp...  19.7 us
    reduce_scatter x1, waiting for transfers between devices, shards(): lax.psum_scatter(jnp.dot(slab, projection, preferred_element_type=jnp.flo...  17.4 us
    all_gather x1, waiting for transfers between devices, shards(): lax.all_gather(grad_out, 'mp', axis=0, tiled=True)  13.2 us
    dot_general x1, matrix products, shards(): jnp.dot(slab, teacher_weight, preferred_element_type=jnp.float32)  10.1 us
    unnamed x5, local copies, waits for them, and re-layouts  9.25 us
  transfers between devices with their start and end apart: 5, of which 5 were waited for; matrix products, arithmetic and copies ran while one was open for 7% of the time, Pallas kernels for 0%

commit v1 on v0

--- a/solution.py
+++ b/solution.py
@@ -1,7 +1,429 @@
+import functools
+
 import jax
 import jax.numpy as jnp
 from jax import lax
+from jax.experimental import pallas as pl
+from jax.experimental.pallas import tpu as pltpu
 from jax.sharding import PartitionSpec as P
+
+MESH = pl.DeviceIdType.MESH
+F32 = jnp.float32
+BF16 = jnp.bfloat16
+TILE = 256
+
+
+def kernel(
+    total_rows,
+    teacher_ref, weight_ref, student_ref, projection_ref, order_ref,
+    cos_ref, dz_ref, st_ref,
+    xbuf, wbuf, acc, stv, obuf, tsend, trecv, ssend, srecv, tf, zf, dzv, stm, statr,
+    x_recv, send_a, send_b, send_x, local_x, local_w, o_send, o_recv,
+    t_send, t_recv, s_send, s_recv, q_send, q_recv, d_send, d_recv, local_st, local_dz,
+):
+    dp, mp = lax.axis_index("dp"), lax.axis_index("mp")
+    z, x = dp // 2, dp % 2
+    ox = 1 - x
+    za = z + 1 - 2 * (z % 2)
+    zb = 3 - z
+    half = z // 2
+    mid = (z + 1) // 2 == 1
+    order = [z, za, 2 - half, 3 - 3 * half]
+    rows, width = xbuf.shape[3], xbuf.shape[4]
+    block = 2 * rows
+    sub = tsend.shape[2]
+    cols = wbuf.shape[2]
+    tiles = cols // TILE
+    groups = 4
+
+    def at(plane, column):
+        return (2 * plane + column, mp)
+
+    def mpd(other):
+        return (dp, other)
+
+    def other_mp(d):
+        return (mp + d) % groups
+
+    def own_src(t):
+        if t < 2:
+            return teacher_ref.at[:, pl.ds(t * width, width)]
+        return student_ref
+
+    w_copies = []
+    x_copies = []
+    for t in range(3):
+        x_copies.append(pltpu.make_async_copy(own_src(t), xbuf.at[t, z, x], local_x.at[t]))
+        src = weight_ref.at[pl.ds(t * width, width), :] if t < 2 else projection_ref
+        w_copies.append(pltpu.make_async_copy(src, wbuf.at[t], local_w.at[t]))
+    for t in range(3):
+        x_copies[t].start()
+        w_copies[t].start()
+
+    barrier = pltpu.get_barrier_semaphore()
+    for d in range(1, 8):
+        pl.semaphore_signal(barrier, inc=1, device_id=((dp + d) % 8, mp), device_id_type=MESH)
+    for d in range(1, groups):
+        pl.semaphore_signal(barrier, inc=1, device_id=mpd(other_mp(d)), device_id_type=MESH)
+    pl.semaphore_wait(barrier, 7 + groups - 1)
+
+    def remote(src, dst, ssem, rsem, device):
+        return pltpu.make_async_remote_copy(
+            src_ref=src, dst_ref=dst, send_sem=ssem, recv_sem=rsem,
+            device_id=device, device_id_type=MESH,
+        )
+
+    def copy_x(t, i):
+        src = own_src(t) if i == 0 else xbuf.at[t, order[i], x]
+        return remote(src, xbuf.at[t, order[i], x], send_x.at[t, i], x_recv.at[t, order[i], x], at(z, ox))
+
+    def copy_a(t, i):
+        if i == 1:
+            src, s, c = xbuf.at[t, z, ox], z, ox
+        else:
+            s, c = order[i], x
+            src = own_src(t) if i == 0 else xbuf.at[t, s, c]
+        return remote(src, xbuf.at[t, s, c], send_a.at[t, i], x_recv.at[t, s, c], at(za, x))
+
+    def copy_b(t, i):
+        s = order[i]
+        src = own_src(t) if i == 0 else xbuf.at[t, s, x]
+        return remote(src, xbuf.at[t, s, x], send_b.at[t, i], x_recv.at[t, s, x], at(zb, x))
+
+    def wait_piece(t, s, c):
+        pltpu.make_async_copy(xbuf.at[t, s, c], xbuf.at[t, s, c], x_recv.at[t, s, c]).wait()
+
+    def own(t):
+        copy_a(t, 0).start()
+
+        @pl.when(mid)
+        def _():
+            copy_b(t, 0).start()
+
+        copy_x(t, 0).start()
+
+    def event(t, i):
+        wait_piece(t, order[i], x)
+
+        @pl.when(mid)
+        def _():
+            (copy_b(t, 1) if i == 1 else copy_a(t, i)).start()
+
+        if not (t == 2 and i == 1):
+            copy_x(t, i).start()
+
+    def other(t, i):
+        wait_piece(t, order[i], ox)
+        if t == 2 and i == 0:
+            copy_a(t, 1).start()
+
+    def lhs(t, s):
+        return xbuf[t, s].reshape(block, width)
+
+    def dot_tile(t, s, cs):
+        return jnp.dot(lhs(t, s), wbuf[t, :, cs], preferred_element_type=F32)
+
+    def tile_loop(body):
+        def step(j, carry):
+            body(pl.ds(pl.multiple_of(j * TILE, TILE), TILE))
+            return carry
+
+        lax.fori_loop(0, tiles, step, 0)
+
+    def teacher_first(i):
+        def body(cs):
+            acc[i, :, cs] = dot_tile(0, order[i], cs)
+
+        tile_loop(body)
+
+    def teacher_second(i):
+        b = order[i]
+
+        def body(cs):
+            part = (acc[i, :, cs] + dot_tile(1, b, cs)).astype(BF16)
+            spread = lax.broadcasted_iota(jnp.int32, (block, block), 0) == jnp.broadcast_to(obuf[b], (block, block))
+            picked = lax.dot_general(
+                jnp.where(spread, 1.0, 0.0).astype(BF16), part, (((0,), (0,)), ((), ())), preferred_element_type=F32
+            )
+            tsend[b, :, :, cs] = picked.astype(BF16).reshape(groups, sub, TILE)
+
+        tile_loop(body)
+        for d in range(1, groups):
+            o = other_mp(d)
+            remote(tsend.at[b, o], trecv.at[mp, b], t_send.at[i, d], t_recv.at[mp, b], mpd(o)).start()
+
+    def student_copy(b):
+        return remote(ssend.at[b], srecv.at[mp], s_send.at[b], s_recv.at[mp], mpd(b))
+
+    def student(i):
+        b = order[i]
+
+        def body(cs):
+            ssend[b, :, cs] = dot_tile(2, b, cs).astype(BF16)
+
+        tile_loop(body)
+
+        @pl.when(mp != b)
+        def _():
+            student_copy(b).start()
+
+    def st_copy(i):
+        b = order[i]
+        return pltpu.make_async_copy(
+            stv.at[b], st_ref.at[:, pl.ds(pl.multiple_of(b * block, block), block)], local_st.at[i]
+        )
+
+    def transpose(i):
+        b = order[i]
+
+        def step(j, carry):
+            ks = pl.ds(pl.multiple_of(j * TILE, TILE), TILE)
+            stv[b, ks, :] = xbuf[2, b, :, :, ks].reshape(block, TILE).T
+            return carry
+
+        lax.fori_loop(0, width // TILE, step, 0)
+        st_copy(i).start()
+
+    obuf[mp] = order_ref[...]
+    o_copies = [
+        remote(order_ref, obuf.at[mp], o_send.at[d], o_recv.at[mp], mpd(other_mp(d))) for d in range(1, groups)
+    ]
+
+    own(0)
+    for c in o_copies:
+        c.start()
+    own(1)
+    event(0, 1)
+    x_copies[0].wait()
+    w_copies[0].wait()
+    other(0, 0)
+    teacher_first(0)
+    event(0, 2)
+    event(1, 1)
+    event(0, 3)
+    x_copies[1].wait()
+    w_copies[1].wait()
+    for d in range(1, groups):
+        o = other_mp(d)
+        pltpu.make_async_copy(obuf.at[o], obuf.at[o], o_recv.at[o]).wait()
+    other(1, 0)
+    teacher_second(0)
+    other(0, 1)
+    teacher_first(1)
+    event(1, 2)
+    own(2)
+    other(0, 2)
+    teacher_first(2)
+    event(1, 3)
+    other(0, 3)
+    teacher_first(3)
+    event(2, 1)
+    other(1, 1)
+    teacher_second(1)
+    event(2, 2)
+    other(1, 2)
+    teacher_second(2)
+    x_copies[2].wait()
+    w_copies[2].wait()
+    other(2, 0)
+    student(0)
+    transpose(0)
+    event(2, 3)
+    other(1, 3)
+    teacher_second(3)
+    other(2, 1)
+    student(1)
+    transpose(1)
+
+    for d in range(1, groups):
+        o = other_mp(d)
+        for b in range(groups):
+            pltpu.make_async_copy(trecv.at[o, b], trecv.at[o, b], t_recv.at[o, b]).wait()
+
+    CH = 16
+    per = sub // CH
+
+    def target_step(r, carry):
+        b, rs = r // per, pl.ds(pl.multiple_of((r % per) * CH, CH), CH)
+        total = tsend[b, mp, rs, :].astype(F32)
+        for d in range(1, groups):
+            total = total + trecv[other_mp(d), b, rs, :].astype(F32)
+        tf[pl.ds(pl.multiple_of(r * CH, CH), CH), :] = total.astype(BF16)
+        return carry
+
+    lax.fori_loop(0, block // CH, target_step, 0)
+
+    other(2, 2)
+    student(2)
+    transpose(2)
+    other(2, 3)
+    student(3)
+    transpose(3)
+
+    for d in range(1, groups):
+        o = other_mp(d)
+        pltpu.make_async_copy(srecv.at[o], srecv.at[o], s_recv.at[o]).wait()
+
+    def stats_step(r, carry):
+        rs = pl.ds(pl.multiple_of(r * CH, CH), CH)
+        zz = ssend[mp, rs, :].astype(F32)
+        for d in range(1, groups):
+            zz = zz + srecv[other_mp(d), rs, :].astype(F32)
+        zf[rs, :] = zz
+        tt = tf[rs, :].astype(F32)
+        lane = lax.broadcasted_iota(jnp.int32, (CH, 128), 1)
+        s0 = jnp.sum(zz * tt, axis=1, keepdims=True)
+        s1 = jnp.sum(zz * zz, axis=1, keepdims=True)
+        s2 = jnp.sum(tt * tt, axis=1, keepdims=True)
+        stm[rs, :] = jnp.where(lane == 0, s0, jnp.where(lane == 1, s1, jnp.where(lane == 2, s2, 0.0)))
+        return carry
+
+    lax.fori_loop(0, block // CH, stats_step, 0)
+    statr[dp] = stm[...].T[0:8, :]
+    q_copies = []
+    for d in range(1, 8):
+        o = (dp + d) % 8
+        q_copies.append(remote(statr.at[dp], statr.at[dp], q_send.at[d], q_recv.at[dp], (o, mp)))
+    for c in q_copies:
+        c.start()
+    for d in range(1, 8):
+        o = (dp + d) % 8
+        pltpu.make_async_copy(statr.at[o], statr.at[o], q_recv.at[o]).wait()
+    sums = statr[0]
+    for s in range(1, 8):
+        sums = sums + statr[s]
+    inner = sums[0:1, :]
+    inv_s = lax.rsqrt(sums[1:2, :] + 1e-06)
+    inv_t = lax.rsqrt(sums[2:3, :] + 1e-06)
+    cos_ref[...] = inner * inv_s * inv_t
+    scale = -1.0 / total_rows
+    on_target = jnp.broadcast_to(scale * (inv_s * inv_t), (block, block))
+    on_student = jnp.broadcast_to(scale * (inner * inv_t * inv_s * inv_s * inv_s), (block, block))
+    row = lax.broadcasted_iota(jnp.int32, (block, block), 0)
+    stm[...] = jnp.where(row == 0, on_target, jnp.where(row == 1, on_student, 0.0)).T
+
+    def dz_step(r, carry):
+        rs = pl.ds(pl.multiple_of(r * CH, CH), CH)
+        coef = stm[rs, :]
+        dzv[rs, :] = (tf[rs, :].astype(F32) * coef[:, 0:1] - zf[rs, :] * coef[:, 1:2]).astype(BF16)
+        return carry
+
+    core = mp + 1 - 2 * (mp % 2)
+    across = (mp + 2) % 4
+    across_core = (core + 2) % 4
+
+    def dz_at(o, h):
+        return dz_ref.at[pl.ds(pl.multiple_of(o * block + h * rows, rows), rows), :]
+
+    finals = []
+    for h in range(2):
+        lax.fori_loop(h * (rows // CH), (h + 1) * (rows // CH), dz_step, 0)
+        src = dzv.at[pl.ds(h * rows, rows), :]
+        far = remote(src, dz_at(mp, h), d_send.at[0, h], d_recv.at[mp, h], mpd(across))
+        near = remote(src, dz_at(mp, h), d_send.at[1, h], d_recv.at[mp, h], mpd(core))
+        mine = pltpu.make_async_copy(src, dz_at(mp, h), local_dz.at[h])
+        far.start()
+        near.start()
+        mine.start()
+        finals += [far, near]
+    for h in range(2):
+        pltpu.make_async_copy(dz_at(across, h), dz_at(across, h), d_recv.at[across, h]).wait()
+        relay = remote(dz_at(across, h), dz_at(across, h), d_send.at[2, h], d_recv.at[across, h], mpd(core))
+        relay.start()
+        finals.append(relay)
+    for h in range(2):
+        for o in (core, across_core):
+            pltpu.make_async_copy(dz_at(o, h), dz_at(o, h), d_recv.at[o, h]).wait()
+        pltpu.make_async_copy(dzv.at[pl.ds(h * rows, rows), :], dz_at(mp, h), local_dz.at[h]).wait()
+
+    for c in finals + q_copies + o_copies:
+        c.wait_send()
+    for t in range(3):
+        copy_a(t, 0).wait_send()
+        for i in range(groups):
+            if not (t == 2 and i == 1):
+                copy_x(t, i).wait_send()
+
+        @pl.when(mid)
+        def _():
+            copy_b(t, 0).wait_send()
+            copy_b(t, 1).wait_send()
+            copy_a(t, 2).wait_send()
+            copy_a(t, 3).wait_send()
+
+    copy_a(2, 1).wait_send()
+    for i in range(groups):
+        b = order[i]
+        for d in range(1, groups):
+            o = other_mp(d)
+            remote(tsend.at[b, o], trecv.at[mp, b], t_send.at[i, d], t_recv.at[mp, b], mpd(o)).wait_send()
+
+        @pl.when(mp != b)
+        def _():
+            student_copy(b).wait_send()
+
+        st_copy(i).wait()
+
+
+def fused_shards(total_rows, teacher_in, teacher_weight, student_in, projection, owner_order):
+    rows, width = student_in.shape
+    cols = projection.shape[1]
+    block = owner_order.shape[0]
+    groups = total_rows // block
+    sub = block // groups
+    any_spec = pl.BlockSpec(memory_space=pl.ANY)
+    vmem_spec = pl.BlockSpec(memory_space=pltpu.VMEM)
+    dma = pltpu.SemaphoreType.DMA
+    cos, dz, st = pl.pallas_call(
+        functools.partial(kernel, total_rows),
+        out_shape=(
+            jax.ShapeDtypeStruct((1, block), F32),
+            jax.ShapeDtypeStruct((total_rows, cols), BF16),
+            jax.ShapeDtypeStruct((width, total_rows), BF16),
+        ),
+        in_specs=[any_spec] * 4 + [vmem_spec],
+        out_specs=(vmem_spec, any_spec, any_spec),
+        scratch_shapes=[
+            pltpu.VMEM((3, 4, 2, rows, width), BF16),
+            pltpu.VMEM((3, width, cols), BF16),
+            pltpu.VMEM((4, block, cols), F32),
+            pltpu.VMEM((4, width, block), BF16),
+            pltpu.VMEM((4, 1, block), jnp.int32),
+            pltpu.VMEM((4, groups, sub, cols), BF16),
+            pltpu.VMEM((4, groups, sub, cols), BF16),
+            pltpu.VMEM((4, block, cols), BF16),
+            pltpu.VMEM((4, block, cols), BF16),
+            pltpu.VMEM((block, cols), BF16),
+            pltpu.VMEM((block, cols), F32),
+            pltpu.VMEM((block, cols), BF16),
+            pltpu.VMEM((block, 128), F32),
+            pltpu.VMEM((8, 8, 128), F32),
+            dma((3, 4, 2)),
+            dma((3, 4)),
+            dma((3, 2)),
+            dma((3, 4)),
+            dma((3,)),
+            dma((3,)),
+            dma((4,)),
+            dma((4,)),
+            dma((4, 4)),
+            dma((4, 4)),
+            dma((4,)),
+            dma((4,)),
+            dma((8,)),
+            dma((8,)),
+            dma((3, 2)),
+            dma((4, 2)),
+            dma((4,)),
+            dma((2,)),
+        ],
+        compiler_params=pltpu.CompilerParams(
+            collective_id=0, has_side_effects=True, vmem_limit_bytes=56 * 1024 * 1024
+        ),
+        name="distill",
+    )(teacher_in, teacher_weight, student_in, projection, owner_order.reshape(1, block))
+    grad = jnp.dot(st, dz, preferred_element_type=F32)
+    return grad, cos.reshape(block)
 
 
 def shards(teacher_in, teacher_weight, student_in, projection, owner_order):
@@ -56,8 +478,16 @@
 
 
 def solution(mesh):
+    fits = mesh.shape["dp"] == 8 and mesh.shape["mp"] == 4
+
+    def step(teacher_in, teacher_weight, student_in, projection, owner_order):
+        args = (teacher_in, teacher_weight, student_in, projection, owner_order)
+        if fits:
+            return fused_shards(owner_order.shape[0] * mesh.shape["mp"], *args)
+        return shards(*args)
+
     return jax.shard_map(
-        shards,
+        step,
         mesh=mesh,
         in_specs=(P("dp", "mp"), P("mp", "dp"), P("dp", "mp"), P("mp", "dp"), P("mp")),
         out_specs=(P("mp", "dp"), P("mp")),

time: 251 us -> 108 us (0.43)
  waiting for transfers between devices: 169 us -> 0 us
  Pallas kernels: 0 us -> 97.4 us
  blocking collectives: 29.8 us -> 0 us
  matrix products: 23.1 us -> 7.6 us
  between operations: 13.8 us -> 0.65 us
  local copies, waits for them, and re-layouts: 11.4 us -> 0.52 us
  other arithmetic: 3.62 us -> 0 us
    all_gather x3 -> x0, waiting for transfers between devices: 130 us -> none  [the longest x1 77.6 us: shards(): teacher_all = lax.all_gather(teacher_in, 'dp', axis=0, tiled=True)]
    pallas_call x0 -> x1, Pallas kernels: none -> 97.4 us  [fused_shards(): pl.pallas_call(functools.partial(kernel, total_rows), out_shape=(jax.Shap...]
    reduce_scatter x2 -> x0, waiting for transfers between devices: 37.1 us -> none  [the longest x1 19.7 us: shards(): lax.psum_scatter(jnp.dot(slab, teacher_weight, preferred_element_type=jnp...]
    psum x1 -> x0, blocking collectives: 21.4 us -> none  [shards(): lax.psum((jnp.sum(student_out * target_f, axis=1), jnp.sum(student_out *...]
    dot_general x3 -> x1, matrix products: 23.1 us -> 7.6 us  [fused_shards(): grad = jnp.dot(st, dz, preferred_element_type=F32)]
    unnamed x5 -> x3, local copies, waits for them, and re-layouts: 9.25 us -> 0.52 us
    all_to_all x1 -> x0, blocking collectives: 8.42 us -> none  [shards(): lax.all_to_all(picked, 'mp', split_axis=0, concat_axis=0, tiled=True)]
  transfers between devices with their start and end apart: 5 -> 0, of which waited for: 5 -> 0; matrix products, arithmetic and copies ran while one was open for 7% -> 0% of each run, Pallas kernels for 0% -> 0%
where the time goes in v1:
time: 108 us; the launch traced here: 106 us
  Pallas kernels  97.4 us (90%)
  matrix products  7.6 us (7%)
    pallas_call x1, Pallas kernels, fused_shards(): pl.pallas_call(functools.partial(kernel, total_rows), out_shape=(jax.Shap...  97.4 us
    dot_general x1, matrix products, fused_shards(): grad = jnp.dot(st, dz, preferred_element_type=F32)  7.6 us

profile of v1, /device:TPU:0, one launch (start us, length us, event | category | flops | bytes accessed | tf_op | source)
XLA Modules:
  0.0 106.1 jit_solution(4135453616877713249)
XLA Ops:
  0.6 97.4 %distill.1 = (f32[1,128]{1,0:T(1,128)}, bf16[512,1024]{1,0:T(8,128)(2,1)}, bf16[2048,512]{1,0:T(8,128)(2,1)}) custom-call(bf16[64,4096]{1,0:T(8,128)(2,1)} %teacher_ref.1, bf16[4096,1024]{1,0:T(8,128)(2,1)} %weight_ref.1, bf16[64,2048]{1,0:T(8,128)(2,1)} %student_ref.1, bf16[2048,1024]{1,0:T(8,128)(2,1)} %projection_ref.1, s32[1,128]{1,0:T(1,128)} %bitcast.4), custom_call_target="tpu_custom_call" | custom-call | tf_op jit(solution)/shard_map/distill/pallas_call | solution.py:377
  98.0 0.0 copy-start
  98.0 7.6 %fusion = f32[2048,1024]{1,0:T(8,128)} fusion(bf16[2048,512]{1,0:T(8,128)(2,1)} %get-tuple-element.5, bf16[512,1024]{1,0:T(8,128)(2,1)} %get-tuple-element.6), kind=kOutput, calls=%fused_computation | convolution fusion | flops 2147483648 | bytes 11534336 | tf_op jit(solution)/shard_map/dot_general | solution.py:425
  105.6 0.0 copy-done
  105.6 0.5 copy.8
Async XLA Ops:
  98.0 7.6 %copy-start = (f32[1,128]{1,0:T(1,128)S(1)}, f32[1,128]{1,0:T(1,128)}, u32[]{:S(2)}) copy-start(f32[1,128]{1,0:T(1,128)} %get-tuple-element.7) | copy-start | bytes 1540

commit v2 on v1

--- a/solution.py
+++ b/solution.py
@@ -17,9 +17,10 @@
     total_rows,
     teacher_ref, weight_ref, student_ref, projection_ref, order_ref,
     cos_ref, dz_ref, st_ref,
-    xbuf, wbuf, acc, stv, obuf, tsend, trecv, ssend, srecv, tf, zf, dzv, stm, statr,
+    xbuf, wbuf, acc, stv, obuf, tsend, trecv, ssend, srecv, tall, zall, dzv, stm, statr, coef,
     x_recv, send_a, send_b, send_x, local_x, local_w, o_send, o_recv,
-    t_send, t_recv, s_send, s_recv, q_send, q_recv, d_send, d_recv, local_st, local_dz,
+    t_send, t_recv, s_send, s_recv, q_send, q_recv, g_send, g_recv, z_send, z_recv, c_send, c_recv,
+    local_st, local_dz,
 ):
     dp, mp = lax.axis_index("dp"), lax.axis_index("mp")
     z, x = dp // 2, dp % 2
@@ -46,15 +47,15 @@
         return (mp + d) % groups
 
     def own_src(t):
-        if t < 2:
-            return teacher_ref.at[:, pl.ds(t * width, width)]
+        if t > 0:
+            return teacher_ref.at[:, pl.ds((t - 1) * width, width)]
         return student_ref
 
     w_copies = []
     x_copies = []
     for t in range(3):
         x_copies.append(pltpu.make_async_copy(own_src(t), xbuf.at[t, z, x], local_x.at[t]))
-        src = weight_ref.at[pl.ds(t * width, width), :] if t < 2 else projection_ref
+        src = weight_ref.at[pl.ds((t - 1) * width, width), :] if t > 0 else projection_ref
         w_copies.append(pltpu.make_async_copy(src, wbuf.at[t], local_w.at[t]))
     for t in range(3):
         x_copies[t].start()
@@ -132,7 +133,7 @@
 
     def teacher_first(i):
         def body(cs):
-            acc[i, :, cs] = dot_tile(0, order[i], cs)
+            acc[i, :, cs] = dot_tile(1, order[i], cs)
 
         tile_loop(body)
 
@@ -140,7 +141,7 @@
         b = order[i]
 
         def body(cs):
-            part = (acc[i, :, cs] + dot_tile(1, b, cs)).astype(BF16)
+            part = (acc[i, :, cs] + dot_tile(2, b, cs)).astype(BF16)
             spread = lax.broadcasted_iota(jnp.int32, (block, block), 0) == jnp.broadcast_to(obuf[b], (block, block))
             picked = lax.dot_general(
                 jnp.where(spread, 1.0, 0.0).astype(BF16), part, (((0,), (0,)), ((), ())), preferred_element_type=F32
@@ -159,7 +160,7 @@
         b = order[i]
 
         def body(cs):
-            ssend[b, :, cs] = dot_tile(2, b, cs).astype(BF16)
+            ssend[b, :, cs] = dot_tile(0, b, cs).astype(BF16)
 
         tile_loop(body)
 
@@ -178,7 +179,7 @@
 
         def step(j, carry):
             ks = pl.ds(pl.multiple_of(j * TILE, TILE), TILE)
-            stv[b, ks, :] = xbuf[2, b, :, :, ks].reshape(block, TILE).T
+            stv[b, ks, :] = xbuf[0, b, :, :, ks].reshape(block, TILE).T
             return carry
 
         lax.fori_loop(0, width // TILE, step, 0)
@@ -188,6 +189,72 @@
     o_copies = [
         remote(order_ref, obuf.at[mp], o_send.at[d], o_recv.at[mp], mpd(other_mp(d))) for d in range(1, groups)
     ]
+
+    CH = 16
+    core = mp + 1 - 2 * (mp % 2)
+    across = (mp + 2) % 4
+    across_core = (core + 2) % 4
+
+    def arrived(ref, sem):
+        pltpu.make_async_copy(ref, ref, sem).wait()
+
+    def z_copy(k):
+        o, to = ((mp, across), (mp, core), (across, core))[k]
+        return remote(zall.at[o], zall.at[o], z_send.at[k], z_recv.at[o], mpd(to))
+
+    def student_sum():
+        for d in range(1, groups):
+            o = other_mp(d)
+            arrived(srecv.at[o], s_recv.at[o])
+
+        def step(r, carry):
+            rs = pl.ds(pl.multiple_of(r * CH, CH), CH)
+            total = ssend[mp, rs, :].astype(F32)
+            for d in range(1, groups):
+                total = total + srecv[other_mp(d), rs, :].astype(F32)
+            zall[mp, rs, :] = total
+            return carry
+
+        lax.fori_loop(0, block // CH, step, 0)
+        z_copy(0).start()
+        z_copy(1).start()
+
+    def student_relay():
+        arrived(zall.at[across], z_recv.at[across])
+        z_copy(2).start()
+
+    def g_copy(i, k):
+        b = order[i]
+        o, to = ((mp, across), (mp, core), (across, core))[k]
+        return remote(tall.at[o, b], tall.at[o, b], g_send.at[i, k], g_recv.at[o, b], mpd(to))
+
+    def target_sum(i):
+        b = order[i]
+        for d in range(1, groups):
+            o = other_mp(d)
+            arrived(trecv.at[o, b], t_recv.at[o, b])
+        for r in range(sub // CH):
+            rs = pl.ds(r * CH, CH)
+            total = tsend[b, mp, rs, :].astype(F32)
+            for d in range(1, groups):
+                total = total + trecv[other_mp(d), b, rs, :].astype(F32)
+            tall[mp, b, rs, :] = total.astype(BF16)
+        g_copy(i, 0).start()
+        g_copy(i, 1).start()
+        for r in range(sub // CH):
+            rows_here = pl.ds(pl.multiple_of(b * sub + r * CH, CH), CH)
+            tt = tall[mp, b, pl.ds(r * CH, CH), :].astype(F32)
+            zz = zall[mp, rows_here, :]
+            lane = lax.broadcasted_iota(jnp.int32, (CH, 128), 1)
+            s0 = jnp.sum(zz * tt, axis=1, keepdims=True)
+            s1 = jnp.sum(zz * zz, axis=1, keepdims=True)
+            s2 = jnp.sum(tt * tt, axis=1, keepdims=True)
+            stm[rows_here, :] = jnp.where(lane == 0, s0, jnp.where(lane == 1, s1, jnp.where(lane == 2, s2, 0.0)))
+
+    def target_relay(i):
+        b = order[i]
+        arrived(tall.at[across, b], g_recv.at[across, b])
+        g_copy(i, 2).start()
 
     own(0)
     for c in o_copies:
@@ -197,88 +264,58 @@
     x_copies[0].wait()
     w_copies[0].wait()
     other(0, 0)
-    teacher_first(0)
+    student(0)
     event(0, 2)
     event(1, 1)
     event(0, 3)
     x_copies[1].wait()
     w_copies[1].wait()
-    for d in range(1, groups):
-        o = other_mp(d)
-        pltpu.make_async_copy(obuf.at[o], obuf.at[o], o_recv.at[o]).wait()
     other(1, 0)
-    teacher_second(0)
+    teacher_first(0)
     other(0, 1)
-    teacher_first(1)
+    student(1)
     event(1, 2)
     own(2)
     other(0, 2)
-    teacher_first(2)
+    student(2)
     event(1, 3)
     other(0, 3)
-    teacher_first(3)
+    student(3)
     event(2, 1)
     other(1, 1)
-    teacher_second(1)
+    teacher_first(1)
     event(2, 2)
+    student_sum()
     other(1, 2)
-    teacher_second(2)
+    teacher_first(2)
     x_copies[2].wait()
     w_copies[2].wait()
-    other(2, 0)
-    student(0)
-    transpose(0)
-    event(2, 3)
-    other(1, 3)
-    teacher_second(3)
-    other(2, 1)
-    student(1)
-    transpose(1)
-
     for d in range(1, groups):
         o = other_mp(d)
-        for b in range(groups):
-            pltpu.make_async_copy(trecv.at[o, b], trecv.at[o, b], t_recv.at[o, b]).wait()
-
-    CH = 16
-    per = sub // CH
-
-    def target_step(r, carry):
-        b, rs = r // per, pl.ds(pl.multiple_of((r % per) * CH, CH), CH)
-        total = tsend[b, mp, rs, :].astype(F32)
-        for d in range(1, groups):
-            total = total + trecv[other_mp(d), b, rs, :].astype(F32)
-        tf[pl.ds(pl.multiple_of(r * CH, CH), CH), :] = total.astype(BF16)
-        return carry
-
-    lax.fori_loop(0, block // CH, target_step, 0)
-
+        arrived(obuf.at[o], o_recv.at[o])
+    other(2, 0)
+    teacher_second(0)
+    event(2, 3)
+    student_relay()
+    transpose(0)
+    transpose(1)
+    other(1, 3)
+    teacher_first(3)
+    transpose(2)
+    transpose(3)
+    other(2, 1)
+    teacher_second(1)
+    target_sum(0)
     other(2, 2)
-    student(2)
-    transpose(2)
+    teacher_second(2)
+    target_sum(1)
+    target_relay(0)
     other(2, 3)
-    student(3)
-    transpose(3)
-
-    for d in range(1, groups):
-        o = other_mp(d)
-        pltpu.make_async_copy(srecv.at[o], srecv.at[o], s_recv.at[o]).wait()
-
-    def stats_step(r, carry):
-        rs = pl.ds(pl.multiple_of(r * CH, CH), CH)
-        zz = ssend[mp, rs, :].astype(F32)
-        for d in range(1, groups):
-            zz = zz + srecv[other_mp(d), rs, :].astype(F32)
-        zf[rs, :] = zz
-        tt = tf[rs, :].astype(F32)
-        lane = lax.broadcasted_iota(jnp.int32, (CH, 128), 1)
-        s0 = jnp.sum(zz * tt, axis=1, keepdims=True)
-        s1 = jnp.sum(zz * zz, axis=1, keepdims=True)
-        s2 = jnp.sum(tt * tt, axis=1, keepdims=True)
-        stm[rs, :] = jnp.where(lane == 0, s0, jnp.where(lane == 1, s1, jnp.where(lane == 2, s2, 0.0)))
-        return carry
-
-    lax.fori_loop(0, block // CH, stats_step, 0)
+    teacher_second(3)
+    target_sum(2)
+    target_relay(1)
+    target_sum(3)
+
     statr[dp] = stm[...].T[0:8, :]
     q_copies = []
     for d in range(1, 8):
@@ -286,9 +323,11 @@
         q_copies.append(remote(statr.at[dp], statr.at[dp], q_send.at[d], q_recv.at[dp], (o, mp)))
     for c in q_copies:
         c.start()
+    target_relay(2)
+    target_relay(3)
     for d in range(1, 8):
         o = (dp + d) % 8
-        pltpu.make_async_copy(statr.at[o], statr.at[o], q_recv.at[o]).wait()
+        arrived(statr.at[o], q_recv.at[o])
     sums = statr[0]
     for s in range(1, 8):
         sums = sums + statr[s]
@@ -297,46 +336,41 @@
     inv_t = lax.rsqrt(sums[2:3, :] + 1e-06)
     cos_ref[...] = inner * inv_s * inv_t
     scale = -1.0 / total_rows
-    on_target = jnp.broadcast_to(scale * (inv_s * inv_t), (block, block))
-    on_student = jnp.broadcast_to(scale * (inner * inv_t * inv_s * inv_s * inv_s), (block, block))
-    row = lax.broadcasted_iota(jnp.int32, (block, block), 0)
-    stm[...] = jnp.where(row == 0, on_target, jnp.where(row == 1, on_student, 0.0)).T
-
-    def dz_step(r, carry):
-        rs = pl.ds(pl.multiple_of(r * CH, CH), CH)
-        coef = stm[rs, :]
-        dzv[rs, :] = (tf[rs, :].astype(F32) * coef[:, 0:1] - zf[rs, :] * coef[:, 1:2]).astype(BF16)
-        return carry
-
-    core = mp + 1 - 2 * (mp % 2)
-    across = (mp + 2) % 4
-    across_core = (core + 2) % 4
-
-    def dz_at(o, h):
-        return dz_ref.at[pl.ds(pl.multiple_of(o * block + h * rows, rows), rows), :]
-
-    finals = []
-    for h in range(2):
-        lax.fori_loop(h * (rows // CH), (h + 1) * (rows // CH), dz_step, 0)
-        src = dzv.at[pl.ds(h * rows, rows), :]
-        far = remote(src, dz_at(mp, h), d_send.at[0, h], d_recv.at[mp, h], mpd(across))
-        near = remote(src, dz_at(mp, h), d_send.at[1, h], d_recv.at[mp, h], mpd(core))
-        mine = pltpu.make_async_copy(src, dz_at(mp, h), local_dz.at[h])
-        far.start()
-        near.start()
-        mine.start()
-        finals += [far, near]
-    for h in range(2):
-        pltpu.make_async_copy(dz_at(across, h), dz_at(across, h), d_recv.at[across, h]).wait()
-        relay = remote(dz_at(across, h), dz_at(across, h), d_send.at[2, h], d_recv.at[across, h], mpd(core))
-        relay.start()
-        finals.append(relay)
-    for h in range(2):
-        for o in (core, across_core):
-            pltpu.make_async_copy(dz_at(o, h), dz_at(o, h), d_recv.at[o, h]).wait()
-        pltpu.make_async_copy(dzv.at[pl.ds(h * rows, rows), :], dz_at(mp, h), local_dz.at[h]).wait()
-
-    for c in finals + q_copies + o_copies:
+    on_target = jnp.broadcast_to(scale * (inv_s * inv_t), (8, block))
+    on_student = jnp.broadcast_to(scale * (inner * inv_t * inv_s * inv_s * inv_s), (8, block))
+    row = lax.broadcasted_iota(jnp.int32, (8, block), 0)
+    coef[mp] = jnp.where(row == 0, on_target, jnp.where(row == 1, on_student, 0.0))
+    c_copies = [
+        remote(coef.at[mp], coef.at[mp], c_send.at[d], c_recv.at[mp], mpd(other_mp(d))) for d in range(1, groups)
+    ]
+    for c in c_copies:
+        c.start()
+
+    def dz_copy(k, o):
+        here = pl.ds(pl.multiple_of(o * block, block), block)
+        return pltpu.make_async_copy(dzv.at[o], dz_ref.at[here, :], local_dz.at[k])
+
+    owners = (mp, core, across, across_core)
+    for k, o in enumerate(owners):
+        if k > 0:
+            arrived(coef.at[o], c_recv.at[o])
+            if k != 2:
+                for b in range(4):
+                    arrived(tall.at[o, b], g_recv.at[o, b])
+                arrived(zall.at[o], z_recv.at[o])
+        stm[...] = jnp.concatenate([coef[o], jnp.zeros((block - 8, block), F32)], axis=0).T
+
+        def dz_step(r, carry):
+            rs = pl.ds(pl.multiple_of(r * CH, CH), CH)
+            b, part = r * CH // sub, pl.ds(pl.multiple_of(r * CH % sub, CH), CH)
+            both = stm[rs, :]
+            dzv[o, rs, :] = (tall[o, b, part, :].astype(F32) * both[:, 0:1] - zall[o, rs, :] * both[:, 1:2]).astype(BF16)
+            return carry
+
+        lax.fori_loop(0, block // CH, dz_step, 0)
+        dz_copy(k, o).start()
+
+    for c in c_copies + q_copies + o_copies + [z_copy(k) for k in range(3)]:
         c.wait_send()
     for t in range(3):
         copy_a(t, 0).wait_send()
@@ -357,12 +391,36 @@
         for d in range(1, groups):
             o = other_mp(d)
             remote(tsend.at[b, o], trecv.at[mp, b], t_send.at[i, d], t_recv.at[mp, b], mpd(o)).wait_send()
+        for k in range(3):
+            g_copy(i, k).wait_send()
 
         @pl.when(mp != b)
         def _():
             student_copy(b).wait_send()
 
         st_copy(i).wait()
+        dz_copy(i, owners[i]).wait()
+
+
+def grad_kernel(st_ref, dz_ref, out_ref):
+    out_ref[...] = jnp.dot(st_ref[...], dz_ref[...], preferred_element_type=F32)
+
+
+def grad_matmul(st, dz):
+    width, depth = st.shape
+    cols = dz.shape[1]
+    return pl.pallas_call(
+        grad_kernel,
+        grid=(width // TILE,),
+        in_specs=[
+            pl.BlockSpec((TILE, depth), lambda i: (i, 0)),
+            pl.BlockSpec((depth, cols), lambda i: (0, 0)),
+        ],
+        out_specs=pl.BlockSpec((TILE, cols), lambda i: (i, 0)),
+        out_shape=jax.ShapeDtypeStruct((width, cols), F32),
+        compiler_params=pltpu.CompilerParams(vmem_limit_bytes=32 * 1024 * 1024),
+        name="grad",
+    )(st, dz)
 
 
 def fused_shards(total_rows, teacher_in, teacher_weight, student_in, projection, owner_order):
@@ -393,11 +451,12 @@
             pltpu.VMEM((4, groups, sub, cols), BF16),
             pltpu.VMEM((4, block, cols), BF16),
             pltpu.VMEM((4, block, cols), BF16),
-            pltpu.VMEM((block, cols), BF16),
-            pltpu.VMEM((block, cols), F32),
-            pltpu.VMEM((block, cols), BF16),
+            pltpu.VMEM((4, groups, sub, cols), BF16),
+            pltpu.VMEM((4, block, cols), F32),
+            pltpu.VMEM((4, block, cols), BF16),
             pltpu.VMEM((block, 128), F32),
             pltpu.VMEM((8, 8, 128), F32),
+            pltpu.VMEM((4, 8, block), F32),
             dma((3, 4, 2)),
             dma((3, 4)),
             dma((3, 2)),
@@ -412,18 +471,21 @@
             dma((4,)),
             dma((8,)),
             dma((8,)),
-            dma((3, 2)),
-            dma((4, 2)),
-            dma((4,)),
-            dma((2,)),
+            dma((4, 3)),
+            dma((4, 4)),
+            dma((3,)),
+            dma((4,)),
+            dma((4,)),
+            dma((4,)),
+            dma((4,)),
+            dma((4,)),
         ],
         compiler_params=pltpu.CompilerParams(
             collective_id=0, has_side_effects=True, vmem_limit_bytes=56 * 1024 * 1024
         ),
         name="distill",
     )(teacher_in, teacher_weight, student_in, projection, owner_order.reshape(1, block))
-    grad = jnp.dot(st, dz, preferred_element_type=F32)
-    return grad, cos.reshape(block)
+    return grad_matmul(st, dz), cos.reshape(block)
 
 
 def shards(teacher_in, teacher_weight, student_in, projection, owner_order):

time: 108 us -> 107 us (level); the launches traced: 106 us -> 106 us
  matrix products: 7.6 us -> 0 us
  Pallas kernels: 97.4 us -> 102 us
  local copies, waits for them, and re-layouts: 0.52 us -> 3.32 us
    dot_general x1 -> x0, matrix products: 7.6 us -> none  [fused_shards(): grad = jnp.dot(st, dz, preferred_element_type=F32)]
    pallas_call x0 -> x1, Pallas kernels: none -> 6.08 us  [grad_matmul(): pl.pallas_call(grad_kernel, grid=(width // TILE,), in_specs=[pl.BlockSpec...]
    unnamed x3 -> x7, local copies, waits for them, and re-layouts: 0.52 us -> 3.32 us
where the time goes in v2:
time: 107 us; the launch traced here: 106 us
  Pallas kernels  102 us (95%)
  local copies, waits for them, and re-layouts  3.32 us (3%)
    pallas_call x1, Pallas kernels, fused_shards(): pl.pallas_call(functools.partial(kernel, total_rows), out_shape=(jax.Shap...  96.3 us
    pallas_call x1, Pallas kernels, grad_matmul(): pl.pallas_call(grad_kernel, grid=(width // TILE,), in_specs=[pl.BlockSpec...  6.08 us
    unnamed x7, local copies, waits for them, and re-layouts  3.32 us

profile of v2, /device:TPU:0, one launch (start us, length us, event | category | flops | bytes accessed | tf_op | source)
XLA Modules:
  0.0 106.4 jit_solution(13047816806760888164)
XLA Ops:
  0.6 96.3 %distill.1 = (f32[1,128]{1,0:T(1,128)}, bf16[512,1024]{1,0:T(8,128)(2,1)}, bf16[2048,512]{1,0:T(8,128)(2,1)}) custom-call(bf16[64,4096]{1,0:T(8,128)(2,1)} %teacher_ref.1, bf16[4096,1024]{1,0:T(8,128)(2,1)} %weight_ref.1, bf16[64,2048]{1,0:T(8,128)(2,1)} %student_ref.1, bf16[2048,1024]{1,0:T(8,128)(2,1)} %projection_ref.1, s32[1,128]{1,0:T(1,128)} %bitcast.2), custom_call_target="tpu_custom_call" | custom-call | tf_op jit(solution)/shard_map/distill/pallas_call | solution.py:435
  96.9 0.0 copy-start.2
  96.9 0.0 copy-start
  97.0 1.6 %copy-done = bf16[2048,512]{1,0:T(8,128)(2,1)S(1)} copy-done((bf16[2048,512]{1,0:T(8,128)(2,1)S(1)}, bf16[2048,512]{1,0:T(8,128)(2,1)}, u32[]{:S(2)}) %copy-start) | copy-done | bytes 2097176
  98.5 0.0 copy-start.1
  98.5 1.2 %copy-done.1 = bf16[512,1024]{1,0:T(8,128)(2,1)S(1)} copy-done((bf16[512,1024]{1,0:T(8,128)(2,1)S(1)}, bf16[512,1024]{1,0:T(8,128)(2,1)}, u32[]{:S(2)}) %copy-start.1) | copy-done | bytes 1048600
  99.8 6.1 %grad.1 = f32[2048,1024]{1,0:T(8,128)} custom-call(bf16[2048,512]{1,0:T(8,128)(2,1)S(1)} %copy-done, bf16[512,1024]{1,0:T(8,128)(2,1)S(1)} %copy-done.1), custom_call_target="tpu_custom_call" | custom-call | tf_op jit(solution)/shard_map/grad/pallas_call | solution.py:412
  105.8 0.0 copy-done.2
  105.8 0.5 copy.8
Async XLA Ops:
  96.9 8.9 %copy-start.2 = (f32[1,128]{1,0:T(1,128)S(1)}, f32[1,128]{1,0:T(1,128)}, u32[]{:S(2)}) copy-start(f32[1,128]{1,0:T(1,128)} %get-tuple-element.7) | copy-start | bytes 1540
  96.9 1.6 %copy-start = (bf16[2048,512]{1,0:T(8,128)(2,1)S(1)}, bf16[2048,512]{1,0:T(8,128)(2,1)}, u32[]{:S(2)}) copy-start(bf16[2048,512]{1,0:T(8,128)(2,1)} %get-tuple-element.5.st_ref) | copy-start | bytes 6291460
  98.5 1.2 %copy-start.1 = (bf16[512,1024]{1,0:T(8,128)(2,1)S(1)}, bf16[512,1024]{1,0:T(8,128)(2,1)}, u32[]{:S(2)}) copy-start(bf16[512,1024]{1,0:T(8,128)(2,1)} %get-tuple-element.6.dz_ref) | copy-start | bytes 3145732

commit v3 on v2

--- a/solution.py
+++ b/solution.py
@@ -118,11 +118,11 @@
         if t == 2 and i == 0:
             copy_a(t, 1).start()
 
-    def lhs(t, s):
-        return xbuf[t, s].reshape(block, width)
-
-    def dot_tile(t, s, cs):
-        return jnp.dot(lhs(t, s), wbuf[t, :, cs], preferred_element_type=F32)
+    bases = [2 * half, 2 - 2 * half]
+
+    def dot_pair(t, p, cs):
+        left = xbuf[t, pl.ds(bases[p], 2)].reshape(2 * block, width)
+        return jnp.dot(left, wbuf[t, :, cs], preferred_element_type=F32)
 
     def tile_loop(body):
         def step(j, carry):
@@ -131,42 +131,62 @@
 
         lax.fori_loop(0, tiles, step, 0)
 
-    def teacher_first(i):
-        def body(cs):
-            acc[i, :, cs] = dot_tile(1, order[i], cs)
-
-        tile_loop(body)
-
-    def teacher_second(i):
-        b = order[i]
-
-        def body(cs):
-            part = (acc[i, :, cs] + dot_tile(2, b, cs)).astype(BF16)
-            spread = lax.broadcasted_iota(jnp.int32, (block, block), 0) == jnp.broadcast_to(obuf[b], (block, block))
-            picked = lax.dot_general(
-                jnp.where(spread, 1.0, 0.0).astype(BF16), part, (((0,), (0,)), ((), ())), preferred_element_type=F32
-            )
-            tsend[b, :, :, cs] = picked.astype(BF16).reshape(groups, sub, TILE)
-
-        tile_loop(body)
+    def spread(b):
+        hit = lax.broadcasted_iota(jnp.int32, (block, block), 0) == jnp.broadcast_to(obuf[b], (block, block))
+        return jnp.where(hit, 1.0, 0.0).astype(BF16)
+
+    def permute(b, part, cs):
+        picked = lax.dot_general(spread(b), part, (((0,), (0,)), ((), ())), preferred_element_type=F32)
+        tsend[b, :, :, cs] = picked.astype(BF16).reshape(groups, sub, TILE)
+
+    def teacher_send(i):
+        b = order[i]
         for d in range(1, groups):
             o = other_mp(d)
             remote(tsend.at[b, o], trecv.at[mp, b], t_send.at[i, d], t_recv.at[mp, b], mpd(o)).start()
 
+    def teacher_first(p):
+        def body(cs):
+            acc[pl.ds(bases[p], 2), :, cs] = dot_pair(1, p, cs).reshape(2, block, TILE)
+
+        tile_loop(body)
+
+    def teacher_pair():
+        b = bases[0]
+
+        def body(cs):
+            part = (acc[pl.ds(b, 2), :, cs].reshape(2 * block, TILE) + dot_pair(2, 0, cs)).astype(BF16)
+            permute(b, part[:block], cs)
+            permute(b + 1, part[block:], cs)
+
+        tile_loop(body)
+        teacher_send(0)
+        teacher_send(1)
+
+    def teacher_second(i):
+        b = order[i]
+
+        def body(cs):
+            new = jnp.dot(xbuf[2, b].reshape(block, width), wbuf[2, :, cs], preferred_element_type=F32)
+            permute(b, (acc[b, :, cs] + new).astype(BF16), cs)
+
+        tile_loop(body)
+        teacher_send(i)
+
     def student_copy(b):
         return remote(ssend.at[b], srecv.at[mp], s_send.at[b], s_recv.at[mp], mpd(b))
 
-    def student(i):
-        b = order[i]
-
+    def student(p):
         def body(cs):
-            ssend[b, :, cs] = dot_tile(0, b, cs).astype(BF16)
+            ssend[pl.ds(bases[p], 2), :, cs] = dot_pair(0, p, cs).astype(BF16).reshape(2, block, TILE)
 
         tile_loop(body)
-
-        @pl.when(mp != b)
-        def _():
-            student_copy(b).start()
+        for i in (2 * p, 2 * p + 1):
+            b = order[i]
+
+            @pl.when(mp != b)
+            def _():
+                student_copy(b).start()
 
     def st_copy(i):
         b = order[i]
@@ -261,59 +281,54 @@
         c.start()
     own(1)
     event(0, 1)
+    event(1, 1)
+    event(0, 2)
+    other(0, 0)
+    event(0, 3)
     x_copies[0].wait()
     w_copies[0].wait()
-    other(0, 0)
+    other(0, 1)
     student(0)
-    event(0, 2)
-    event(1, 1)
-    event(0, 3)
+    event(1, 2)
+    own(2)
     x_copies[1].wait()
     w_copies[1].wait()
     other(1, 0)
+    other(1, 1)
     teacher_first(0)
-    other(0, 1)
+    event(1, 3)
+    other(0, 2)
+    other(0, 3)
     student(1)
-    event(1, 2)
-    own(2)
-    other(0, 2)
-    student(2)
-    event(1, 3)
-    other(0, 3)
-    student(3)
     event(2, 1)
-    other(1, 1)
-    teacher_first(1)
+    transpose(0)
+    transpose(1)
+    other(2, 0)
     event(2, 2)
     student_sum()
+    transpose(2)
+    transpose(3)
+    event(2, 3)
     other(1, 2)
-    teacher_first(2)
+    other(1, 3)
+    teacher_first(1)
+    student_relay()
     x_copies[2].wait()
     w_copies[2].wait()
     for d in range(1, groups):
         o = other_mp(d)
         arrived(obuf.at[o], o_recv.at[o])
-    other(2, 0)
-    teacher_second(0)
-    event(2, 3)
-    student_relay()
-    transpose(0)
-    transpose(1)
-    other(1, 3)
-    teacher_first(3)
-    transpose(2)
-    transpose(3)
     other(2, 1)
-    teacher_second(1)
+    teacher_pair()
     target_sum(0)
+    target_sum(1)
     other(2, 2)
     teacher_second(2)
-    target_sum(1)
     target_relay(0)
+    target_relay(1)
     other(2, 3)
     teacher_second(3)
     target_sum(2)
-    target_relay(1)
     target_sum(3)
 
     statr[dp] = stm[...].T[0:8, :]
@@ -402,23 +417,55 @@
         dz_copy(i, owners[i]).wait()
 
 
-def grad_kernel(st_ref, dz_ref, out_ref):
-    out_ref[...] = jnp.dot(st_ref[...], dz_ref[...], preferred_element_type=F32)
+def grad_kernel(st_ref, dz_ref, out_ref, st, dz, out, load, dz_load, store):
+    steps = st.shape[0]
+
+    def rows(j):
+        return pl.ds(pl.multiple_of(j * TILE, TILE), TILE)
+
+    def fetch(j):
+        return pltpu.make_async_copy(st_ref.at[rows(j), :], st.at[j], load.at[j])
+
+    def put(j):
+        return pltpu.make_async_copy(out.at[j], out_ref.at[rows(j), :], store.at[j])
+
+    whole = pltpu.make_async_copy(dz_ref, dz, dz_load)
+    whole.start()
+    for j in range(steps):
+        fetch(j).start()
+    whole.wait()
+
+    def step(j, carry):
+        fetch(j).wait()
+        out[j] = jnp.dot(st[j], dz[...], preferred_element_type=F32)
+        put(j).start()
+        return carry
+
+    lax.fori_loop(0, steps, step, 0)
+    for j in range(steps):
+        put(j).wait()
 
 
 def grad_matmul(st, dz):
     width, depth = st.shape
     cols = dz.shape[1]
+    steps = width // TILE
+    any_spec = pl.BlockSpec(memory_space=pl.ANY)
+    dma = pltpu.SemaphoreType.DMA
     return pl.pallas_call(
         grad_kernel,
-        grid=(width // TILE,),
-        in_specs=[
-            pl.BlockSpec((TILE, depth), lambda i: (i, 0)),
-            pl.BlockSpec((depth, cols), lambda i: (0, 0)),
+        in_specs=[any_spec, any_spec],
+        out_specs=any_spec,
+        out_shape=jax.ShapeDtypeStruct((width, cols), F32),
+        scratch_shapes=[
+            pltpu.VMEM((steps, TILE, depth), BF16),
+            pltpu.VMEM((depth, cols), BF16),
+            pltpu.VMEM((steps, TILE, cols), F32),
+            dma((steps,)),
+            dma(()),
+            dma((steps,)),
         ],
-        out_specs=pl.BlockSpec((TILE, cols), lambda i: (i, 0)),
-        out_shape=jax.ShapeDtypeStruct((width, cols), F32),
-        compiler_params=pltpu.CompilerParams(vmem_limit_bytes=32 * 1024 * 1024),
+        compiler_params=pltpu.CompilerParams(vmem_limit_bytes=56 * 1024 * 1024),
         name="grad",
     )(st, dz)
 

time: 107 us -> 115 us (1.075)
  Pallas kernels: 102 us -> 113 us
  local copies, waits for them, and re-layouts: 3.32 us -> 0.52 us
    pallas_call x1, Pallas kernels: 96.3 us -> 107 us  [fused_shards(): pl.pallas_call(functools.partial(kernel, total_rows), out_shape=(jax.Shap...]
    unnamed x7 -> x3, local copies, waits for them, and re-layouts: 3.32 us -> 0.52 us
where the time goes in v3:
time: 115 us
  Pallas kernels  113 us (98%)
    pallas_call x1, Pallas kernels, fused_shards(): pl.pallas_call(functools.partial(kernel, total_rows), out_shape=(jax.Shap...  107 us
    pallas_call x1, Pallas kernels, grad_matmul(): pl.pallas_call(grad_kernel, in_specs=[any_spec, any_spec], out_specs=any_...  6.44 us

profile of v3, /device:TPU:0, one launch (start us, length us, event | category | flops | bytes accessed | tf_op | source)
XLA Modules:
  0.0 114.5 jit_solution(7712110443416395166)
XLA Ops:
  0.6 106.9 %distill.1 = (f32[1,128]{1,0:T(1,128)}, bf16[512,1024]{1,0:T(8,128)(2,1)}, bf16[2048,512]{1,0:T(8,128)(2,1)}) custom-call(bf16[64,4096]{1,0:T(8,128)(2,1)} %teacher_ref.1, bf16[4096,1024]{1,0:T(8,128)(2,1)} %weight_ref.1, bf16[64,2048]{1,0:T(8,128)(2,1)} %student_ref.1, bf16[2048,1024]{1,0:T(8,128)(2,1)} %projection_ref.1, s32[1,128]{1,0:T(1,128)} %bitcast.2), custom_call_target="tpu_custom_call" | custom-call | tf_op jit(solution)/shard_map/distill/pallas_call | solution.py:482
  107.5 0.0 copy-start
  107.5 6.4 %grad.1 = f32[2048,1024]{1,0:T(8,128)} custom-call(bf16[2048,512]{1,0:T(8,128)(2,1)} %get-tuple-element.5.st_ref, bf16[512,1024]{1,0:T(8,128)(2,1)} %get-tuple-element.6.dz_ref), custom_call_target="tpu_custom_call" | custom-call | tf_op jit(solution)/shard_map/grad/pallas_call | solution.py:455
  114.0 0.0 copy-done
  114.0 0.5 copy.8
Async XLA Ops:
  107.5 6.5 %copy-start = (f32[1,128]{1,0:T(1,128)S(1)}, f32[1,128]{1,0:T(1,128)}, u32[]{:S(2)}) copy-start(f32[1,128]{1,0:T(1,128)} %get-tuple-element.7) | copy-start | bytes 1540

commit v4 on v3

--- a/solution.py
+++ b/solution.py
@@ -78,37 +78,36 @@
         src = own_src(t) if i == 0 else xbuf.at[t, order[i], x]
         return remote(src, xbuf.at[t, order[i], x], send_x.at[t, i], x_recv.at[t, order[i], x], at(z, ox))
 
-    def copy_a(t, i):
-        if i == 1:
-            src, s, c = xbuf.at[t, z, ox], z, ox
-        else:
-            s, c = order[i], x
-            src = own_src(t) if i == 0 else xbuf.at[t, s, c]
-        return remote(src, xbuf.at[t, s, c], send_a.at[t, i], x_recv.at[t, s, c], at(za, x))
-
-    def copy_b(t, i):
-        s = order[i]
-        src = own_src(t) if i == 0 else xbuf.at[t, s, x]
-        return remote(src, xbuf.at[t, s, x], send_b.at[t, i], x_recv.at[t, s, x], at(zb, x))
+    def copy_own(t, k):
+        return remote(own_src(t), xbuf.at[t, z, x], send_a.at[t, k], x_recv.at[t, z, x], at(order[k], x))
+
+    def copy_on(t):
+        src = xbuf.at[t, zb, x]
+        return remote(src, src, send_a.at[t, 0], x_recv.at[t, zb, x], at(za, x))
+
+    def copy_swap(t):
+        src = xbuf.at[t, z, ox]
+        return remote(src, src, send_b.at[t], x_recv.at[t, z, ox], at(za, x))
 
     def wait_piece(t, s, c):
         pltpu.make_async_copy(xbuf.at[t, s, c], xbuf.at[t, s, c], x_recv.at[t, s, c]).wait()
 
     def own(t):
-        copy_a(t, 0).start()
-
-        @pl.when(mid)
+        copy_own(t, 1).start()
+        copy_x(t, 0).start()
+        copy_own(t, 2).start()
+
+        @pl.when(jnp.logical_not(mid))
         def _():
-            copy_b(t, 0).start()
-
-        copy_x(t, 0).start()
+            copy_own(t, 3).start()
 
     def event(t, i):
         wait_piece(t, order[i], x)
-
-        @pl.when(mid)
-        def _():
-            (copy_b(t, 1) if i == 1 else copy_a(t, i)).start()
+        if i == 2:
+
+            @pl.when(mid)
+            def _():
+                copy_on(t).start()
 
         if not (t == 2 and i == 1):
             copy_x(t, i).start()
@@ -116,7 +115,7 @@
     def other(t, i):
         wait_piece(t, order[i], ox)
         if t == 2 and i == 0:
-            copy_a(t, 1).start()
+            copy_swap(t).start()
 
     bases = [2 * half, 2 - 2 * half]
 
@@ -150,18 +149,6 @@
             acc[pl.ds(bases[p], 2), :, cs] = dot_pair(1, p, cs).reshape(2, block, TILE)
 
         tile_loop(body)
-
-    def teacher_pair():
-        b = bases[0]
-
-        def body(cs):
-            part = (acc[pl.ds(b, 2), :, cs].reshape(2 * block, TILE) + dot_pair(2, 0, cs)).astype(BF16)
-            permute(b, part[:block], cs)
-            permute(b + 1, part[block:], cs)
-
-        tile_loop(body)
-        teacher_send(0)
-        teacher_send(1)
 
     def teacher_second(i):
         b = order[i]
@@ -283,43 +270,44 @@
     event(0, 1)
     event(1, 1)
     event(0, 2)
-    other(0, 0)
     event(0, 3)
+    own(2)
     x_copies[0].wait()
     w_copies[0].wait()
+    other(0, 0)
     other(0, 1)
     student(0)
-    event(1, 2)
-    own(2)
     x_copies[1].wait()
     w_copies[1].wait()
     other(1, 0)
     other(1, 1)
     teacher_first(0)
+    event(1, 2)
     event(1, 3)
     other(0, 2)
     other(0, 3)
     student(1)
-    event(2, 1)
-    transpose(0)
-    transpose(1)
-    other(2, 0)
-    event(2, 2)
-    student_sum()
-    transpose(2)
-    transpose(3)
-    event(2, 3)
-    other(1, 2)
-    other(1, 3)
-    teacher_first(1)
-    student_relay()
     x_copies[2].wait()
     w_copies[2].wait()
     for d in range(1, groups):
         o = other_mp(d)
         arrived(obuf.at[o], o_recv.at[o])
+    other(2, 0)
+    event(2, 2)
+    teacher_second(0)
+    student_sum()
+    event(2, 3)
+    transpose(0)
+    transpose(1)
+    transpose(2)
+    transpose(3)
+    student_relay()
+    other(1, 2)
+    other(1, 3)
+    teacher_first(1)
+    event(2, 1)
     other(2, 1)
-    teacher_pair()
+    teacher_second(1)
     target_sum(0)
     target_sum(1)
     other(2, 2)
@@ -388,19 +376,21 @@
     for c in c_copies + q_copies + o_copies + [z_copy(k) for k in range(3)]:
         c.wait_send()
     for t in range(3):
-        copy_a(t, 0).wait_send()
+        copy_own(t, 1).wait_send()
+        copy_own(t, 2).wait_send()
         for i in range(groups):
             if not (t == 2 and i == 1):
                 copy_x(t, i).wait_send()
 
         @pl.when(mid)
         def _():
-            copy_b(t, 0).wait_send()
-            copy_b(t, 1).wait_send()
-            copy_a(t, 2).wait_send()
-            copy_a(t, 3).wait_send()
-
-    copy_a(2, 1).wait_send()
+            copy_on(t).wait_send()
+
+        @pl.when(jnp.logical_not(mid))
+        def _():
+            copy_own(t, 3).wait_send()
+
+    copy_swap(2).wait_send()
     for i in range(groups):
         b = order[i]
         for d in range(1, groups):
@@ -506,7 +496,7 @@
             pltpu.VMEM((4, 8, block), F32),
             dma((3, 4, 2)),
             dma((3, 4)),
-            dma((3, 2)),
+            dma((3,)),
             dma((3, 4)),
             dma((3,)),
             dma((3,)),

time: 115 us -> 123 us (1.070)
  Pallas kernels: 113 us -> 122 us
    pallas_call x1, Pallas kernels: 107 us -> 116 us  [fused_shards(): pl.pallas_call(functools.partial(kernel, total_rows), out_shape=(jax.Shap...]
where the time goes in v4:
time: 123 us
  Pallas kernels  122 us (99%)
    pallas_call x1, Pallas kernels, fused_shards(): pl.pallas_call(functools.partial(kernel, total_rows), out_shape=(jax.Shap...  116 us
    pallas_call x1, Pallas kernels, grad_matmul(): pl.pallas_call(grad_kernel, in_specs=[any_spec, any_spec], out_specs=any_...  6.44 us

profile of v4, /device:TPU:0, one launch (start us, length us, event | category | flops | bytes accessed | tf_op | source)
XLA Modules:
  0.0 123.3 jit_solution(17741623092020904213)
XLA Ops:
  0.6 115.6 %distill.1 = (f32[1,128]{1,0:T(1,128)}, bf16[512,1024]{1,0:T(8,128)(2,1)}, bf16[2048,512]{1,0:T(8,128)(2,1)}) custom-call(bf16[64,4096]{1,0:T(8,128)(2,1)} %teacher_ref.1, bf16[4096,1024]{1,0:T(8,128)(2,1)} %weight_ref.1, bf16[64,2048]{1,0:T(8,128)(2,1)} %student_ref.1, bf16[2048,1024]{1,0:T(8,128)(2,1)} %projection_ref.1, s32[1,128]{1,0:T(1,128)} %bitcast.2), custom_call_target="tpu_custom_call" | custom-call | tf_op jit(solution)/shard_map/distill/pallas_call | solution.py:472
  116.3 0.0 copy-start
  116.3 6.4 %grad.1 = f32[2048,1024]{1,0:T(8,128)} custom-call(bf16[2048,512]{1,0:T(8,128)(2,1)} %get-tuple-element.5.st_ref, bf16[512,1024]{1,0:T(8,128)(2,1)} %get-tuple-element.6.dz_ref), custom_call_target="tpu_custom_call" | custom-call | tf_op jit(solution)/shard_map/grad/pallas_call | solution.py:445
  122.7 0.0 copy-done
  122.7 0.5 copy.8
Async XLA Ops:
  116.3 6.5 %copy-start = (f32[1,128]{1,0:T(1,128)S(1)}, f32[1,128]{1,0:T(1,128)}, u32[]{:S(2)}) copy-start(f32[1,128]{1,0:T(1,128)} %get-tuple-element.7) | copy-start | bytes 1540

commit v5 on v3

--- a/solution.py
+++ b/solution.py
@@ -94,29 +94,19 @@
     def wait_piece(t, s, c):
         pltpu.make_async_copy(xbuf.at[t, s, c], xbuf.at[t, s, c], x_recv.at[t, s, c]).wait()
 
-    def own(t):
-        copy_a(t, 0).start()
-
-        @pl.when(mid)
+    def if_mid(copy, flag=True):
+        @pl.when(mid if flag else jnp.logical_not(mid))
         def _():
-            copy_b(t, 0).start()
-
-        copy_x(t, 0).start()
+            copy.start()
 
     def event(t, i):
         wait_piece(t, order[i], x)
-
-        @pl.when(mid)
-        def _():
-            (copy_b(t, 1) if i == 1 else copy_a(t, i)).start()
-
+        if_mid(copy_b(t, 1) if i == 1 else copy_a(t, i))
         if not (t == 2 and i == 1):
             copy_x(t, i).start()
 
     def other(t, i):
         wait_piece(t, order[i], ox)
-        if t == 2 and i == 0:
-            copy_a(t, 1).start()
 
     bases = [2 * half, 2 - 2 * half]
 
@@ -150,18 +140,6 @@
             acc[pl.ds(bases[p], 2), :, cs] = dot_pair(1, p, cs).reshape(2, block, TILE)
 
         tile_loop(body)
-
-    def teacher_pair():
-        b = bases[0]
-
-        def body(cs):
-            part = (acc[pl.ds(b, 2), :, cs].reshape(2 * block, TILE) + dot_pair(2, 0, cs)).astype(BF16)
-            permute(b, part[:block], cs)
-            permute(b + 1, part[block:], cs)
-
-        tile_loop(body)
-        teacher_send(0)
-        teacher_send(1)
 
     def teacher_second(i):
         b = order[i]
@@ -276,50 +254,69 @@
         arrived(tall.at[across, b], g_recv.at[across, b])
         g_copy(i, 2).start()
 
-    own(0)
+    copy_a(0, 0).start()
+    if_mid(copy_b(0, 0))
+    for t in range(3):
+        copy_x(t, 0).start()
     for c in o_copies:
         c.start()
-    own(1)
     event(0, 1)
-    event(1, 1)
+    if_mid(copy_a(1, 0), False)
     event(0, 2)
-    other(0, 0)
+    if_mid(copy_b(1, 0))
     event(0, 3)
+    if_mid(copy_a(1, 0))
     x_copies[0].wait()
     w_copies[0].wait()
+    other(0, 0)
+    event(1, 1)
+    if_mid(copy_a(2, 0), False)
     other(0, 1)
     student(0)
     event(1, 2)
-    own(2)
+    if_mid(copy_b(2, 0))
+    event(1, 3)
+    other(0, 2)
+    other(0, 3)
+    student(1)
+
+    @pl.when(mid)
+    def _():
+        wait_piece(2, order[1], x)
+        copy_b(2, 1).start()
+
+    event(2, 2)
     x_copies[1].wait()
     w_copies[1].wait()
     other(1, 0)
     other(1, 1)
     teacher_first(0)
-    event(1, 3)
-    other(0, 2)
-    other(0, 3)
-    student(1)
-    event(2, 1)
-    transpose(0)
-    transpose(1)
     other(2, 0)
-    event(2, 2)
-    student_sum()
-    transpose(2)
-    transpose(3)
     event(2, 3)
-    other(1, 2)
-    other(1, 3)
-    teacher_first(1)
-    student_relay()
+    if_mid(copy_a(2, 0))
+    copy_a(2, 1).start()
     x_copies[2].wait()
     w_copies[2].wait()
     for d in range(1, groups):
         o = other_mp(d)
         arrived(obuf.at[o], o_recv.at[o])
+    teacher_second(0)
+    student_sum()
+    transpose(0)
+    transpose(1)
+    transpose(2)
+    transpose(3)
+    student_relay()
+    other(1, 2)
+    other(1, 3)
+    teacher_first(1)
+
+    @pl.when(jnp.logical_not(mid))
+    def _():
+        wait_piece(2, order[1], x)
+
     other(2, 1)
-    teacher_pair()
+    teacher_second(1)
     target_sum(0)
     target_sum(1)
     other(2, 2)

time: 115 us -> 109 us (0.948)
  Pallas kernels: 113 us -> 108 us
    pallas_call x1, Pallas kernels: 107 us -> 101 us  [fused_shards(): pl.pallas_call(functools.partial(kernel, total_rows), out_shape=(jax.Shap...]
where the time goes in v5:
time: 109 us
  Pallas kernels  108 us (99%)
    pallas_call x1, Pallas kernels, fused_shards(): pl.pallas_call(functools.partial(kernel, total_rows), out_shape=(jax.Shap...  101 us
    pallas_call x1, Pallas kernels, grad_matmul(): pl.pallas_call(grad_kernel, in_specs=[any_spec, any_spec], out_specs=any_...  6.44 us

profile of v5, /device:TPU:0, one launch (start us, length us, event | category | flops | bytes accessed | tf_op | source)
XLA Modules:
  0.0 109.0 jit_solution(10909017040829016407)
XLA Ops:
  0.6 101.3 %distill.1 = (f32[1,128]{1,0:T(1,128)}, bf16[512,1024]{1,0:T(8,128)(2,1)}, bf16[2048,512]{1,0:T(8,128)(2,1)}) custom-call(bf16[64,4096]{1,0:T(8,128)(2,1)} %teacher_ref.1, bf16[4096,1024]{1,0:T(8,128)(2,1)} %weight_ref.1, bf16[64,2048]{1,0:T(8,128)(2,1)} %student_ref.1, bf16[2048,1024]{1,0:T(8,128)(2,1)} %projection_ref.1, s32[1,128]{1,0:T(1,128)} %bitcast.2), custom_call_target="tpu_custom_call" | custom-call | tf_op jit(solution)/shard_map/distill/pallas_call | solution.py:479
  102.0 0.0 copy-start
  102.0 6.4 %grad.1 = f32[2048,1024]{1,0:T(8,128)} custom-call(bf16[2048,512]{1,0:T(8,128)(2,1)} %get-tuple-element.5.st_ref, bf16[512,1024]{1,0:T(8,128)(2,1)} %get-tuple-element.6.dz_ref), custom_call_target="tpu_custom_call" | custom-call | tf_op jit(solution)/shard_map/grad/pallas_call | solution.py:452
  108.4 0.0 copy-done
  108.4 0.5 copy.8
Async XLA Ops:
  102.0 6.5 %copy-start = (f32[1,128]{1,0:T(1,128)S(1)}, f32[1,128]{1,0:T(1,128)}, u32[]{:S(2)}) copy-start(f32[1,128]{1,0:T(1,128)} %get-tuple-element.7) | copy-start | bytes 1540

commit v6 on v2

--- a/solution.py
+++ b/solution.py
@@ -101,8 +101,6 @@
         def _():
             copy_b(t, 0).start()
 
-        copy_x(t, 0).start()
-
     def event(t, i):
         wait_piece(t, order[i], x)
 
@@ -118,11 +116,8 @@
         if t == 2 and i == 0:
             copy_a(t, 1).start()
 
-    def lhs(t, s):
-        return xbuf[t, s].reshape(block, width)
-
-    def dot_tile(t, s, cs):
-        return jnp.dot(lhs(t, s), wbuf[t, :, cs], preferred_element_type=F32)
+    def dot_block(t, b, cs):
+        return jnp.dot(xbuf[t, b].reshape(block, width), wbuf[t, :, cs], preferred_element_type=F32)
 
     def tile_loop(body):
         def step(j, carry):
@@ -131,28 +126,37 @@
 
         lax.fori_loop(0, tiles, step, 0)
 
-    def teacher_first(i):
-        def body(cs):
-            acc[i, :, cs] = dot_tile(1, order[i], cs)
-
-        tile_loop(body)
-
-    def teacher_second(i):
-        b = order[i]
-
-        def body(cs):
-            part = (acc[i, :, cs] + dot_tile(2, b, cs)).astype(BF16)
-            spread = lax.broadcasted_iota(jnp.int32, (block, block), 0) == jnp.broadcast_to(obuf[b], (block, block))
-            picked = lax.dot_general(
-                jnp.where(spread, 1.0, 0.0).astype(BF16), part, (((0,), (0,)), ((), ())), preferred_element_type=F32
-            )
-            tsend[b, :, :, cs] = picked.astype(BF16).reshape(groups, sub, TILE)
-
-        tile_loop(body)
+    def spread(b):
+        hit = lax.broadcasted_iota(jnp.int32, (block, block), 0) == jnp.broadcast_to(obuf[b], (block, block))
+        return jnp.where(hit, 1.0, 0.0).astype(BF16)
+
+    def permute(b, part, cs):
+        picked = lax.dot_general(spread(b), part, (((0,), (0,)), ((), ())), preferred_element_type=F32)
+        tsend[b, :, :, cs] = picked.astype(BF16).reshape(groups, sub, TILE)
+
+    def teacher_send(i):
+        b = order[i]
         for d in range(1, groups):
             o = other_mp(d)
             remote(tsend.at[b, o], trecv.at[mp, b], t_send.at[i, d], t_recv.at[mp, b], mpd(o)).start()
 
+    def teacher_first(i):
+        b = order[i]
+
+        def body(cs):
+            acc[b, :, cs] = dot_block(1, b, cs)
+
+        tile_loop(body)
+
+    def teacher_second(i):
+        b = order[i]
+
+        def body(cs):
+            permute(b, (acc[b, :, cs] + dot_block(2, b, cs)).astype(BF16), cs)
+
+        tile_loop(body)
+        teacher_send(i)
+
     def student_copy(b):
         return remote(ssend.at[b], srecv.at[mp], s_send.at[b], s_recv.at[mp], mpd(b))
 
@@ -160,7 +164,7 @@
         b = order[i]
 
         def body(cs):
-            ssend[b, :, cs] = dot_tile(0, b, cs).astype(BF16)
+            ssend[b, :, cs] = dot_block(0, b, cs).astype(BF16)
 
         tile_loop(body)
 
@@ -257,9 +261,12 @@
         g_copy(i, 2).start()
 
     own(0)
+    copy_x(0, 0).start()
+    copy_x(1, 0).start()
     for c in o_copies:
         c.start()
     own(1)
+    copy_x(2, 0).start()
     event(0, 1)
     x_copies[0].wait()
     w_copies[0].wait()
@@ -282,6 +289,7 @@
     other(0, 3)
     student(3)
     event(2, 1)
+    other(2, 0)
     other(1, 1)
     teacher_first(1)
     event(2, 2)
@@ -293,16 +301,11 @@
     for d in range(1, groups):
         o = other_mp(d)
         arrived(obuf.at[o], o_recv.at[o])
-    other(2, 0)
     teacher_second(0)
     event(2, 3)
     student_relay()
-    transpose(0)
-    transpose(1)
     other(1, 3)
     teacher_first(3)
-    transpose(2)
-    transpose(3)
     other(2, 1)
     teacher_second(1)
     target_sum(0)
@@ -314,6 +317,8 @@
     teacher_second(3)
     target_sum(2)
     target_relay(1)
+    transpose(0)
+    transpose(1)
     target_sum(3)
 
     statr[dp] = stm[...].T[0:8, :]
@@ -324,7 +329,9 @@
     for c in q_copies:
         c.start()
     target_relay(2)
+    transpose(2)
     target_relay(3)
+    transpose(3)
     for d in range(1, 8):
         o = (dp + d) % 8
         arrived(statr.at[o], q_recv.at[o])
@@ -402,23 +409,55 @@
         dz_copy(i, owners[i]).wait()
 
 
-def grad_kernel(st_ref, dz_ref, out_ref):
-    out_ref[...] = jnp.dot(st_ref[...], dz_ref[...], preferred_element_type=F32)
+def grad_kernel(st_ref, dz_ref, out_ref, st, dz, out, load, dz_load, store):
+    steps = st.shape[0]
+
+    def rows(j):
+        return pl.ds(pl.multiple_of(j * TILE, TILE), TILE)
+
+    def fetch(j):
+        return pltpu.make_async_copy(st_ref.at[rows(j), :], st.at[j], load.at[j])
+
+    def put(j):
+        return pltpu.make_async_copy(out.at[j], out_ref.at[rows(j), :], store.at[j])
+
+    whole = pltpu.make_async_copy(dz_ref, dz, dz_load)
+    whole.start()
+    for j in range(steps):
+        fetch(j).start()
+    whole.wait()
+
+    def step(j, carry):
+        fetch(j).wait()
+        out[j] = jnp.dot(st[j], dz[...], preferred_element_type=F32)
+        put(j).start()
+        return carry
+
+    lax.fori_loop(0, steps, step, 0)
+    for j in range(steps):
+        put(j).wait()
 
 
 def grad_matmul(st, dz):
     width, depth = st.shape
     cols = dz.shape[1]
+    steps = width // TILE
+    any_spec = pl.BlockSpec(memory_space=pl.ANY)
+    dma = pltpu.SemaphoreType.DMA
     return pl.pallas_call(
         grad_kernel,
-        grid=(width // TILE,),
-        in_specs=[
-            pl.BlockSpec((TILE, depth), lambda i: (i, 0)),
-            pl.BlockSpec((depth, cols), lambda i: (0, 0)),
+        in_specs=[any_spec, any_spec],
+        out_specs=any_spec,
+        out_shape=jax.ShapeDtypeStruct((width, cols), F32),
+        scratch_shapes=[
+            pltpu.VMEM((steps, TILE, depth), BF16),
+            pltpu.VMEM((depth, cols), BF16),
+            pltpu.VMEM((steps, TILE, cols), F32),
+            dma((steps,)),
+            dma(()),
+            dma((steps,)),
         ],
-        out_specs=pl.BlockSpec((TILE, cols), lambda i: (i, 0)),
-        out_shape=jax.ShapeDtypeStruct((width, cols), F32),
-        compiler_params=pltpu.CompilerParams(vmem_limit_bytes=32 * 1024 * 1024),
+        compiler_params=pltpu.CompilerParams(vmem_limit_bytes=56 * 1024 * 1024),
         name="grad",
     )(st, dz)
 

time: 107 us -> 110 us (1.028)
  Pallas kernels: 102 us -> 109 us
  local copies, waits for them, and re-layouts: 3.32 us -> 0.52 us
    pallas_call x1, Pallas kernels: 96.3 us -> 102 us  [fused_shards(): pl.pallas_call(functools.partial(kernel, total_rows), out_shape=(jax.Shap...]
    unnamed x7 -> x3, local copies, waits for them, and re-layouts: 3.32 us -> 0.52 us
where the time goes in v6:
time: 110 us
  Pallas kernels  109 us (99%)
    pallas_call x1, Pallas kernels, fused_shards(): pl.pallas_call(functools.partial(kernel, total_rows), out_shape=(jax.Shap...  102 us
    pallas_call x1, Pallas kernels, grad_matmul(): pl.pallas_call(grad_kernel, in_specs=[any_spec, any_spec], out_specs=any_...  6.44 us

profile of v6, /device:TPU:0, one launch (start us, length us, event | category | flops | bytes accessed | tf_op | source)
XLA Modules:
  0.0 109.7 jit_solution(7174881033844674086)
XLA Ops:
  0.6 102.1 %distill.1 = (f32[1,128]{1,0:T(1,128)}, bf16[512,1024]{1,0:T(8,128)(2,1)}, bf16[2048,512]{1,0:T(8,128)(2,1)}) custom-call(bf16[64,4096]{1,0:T(8,128)(2,1)} %teacher_ref.1, bf16[4096,1024]{1,0:T(8,128)(2,1)} %weight_ref.1, bf16[64,2048]{1,0:T(8,128)(2,1)} %student_ref.1, bf16[2048,1024]{1,0:T(8,128)(2,1)} %projection_ref.1, s32[1,128]{1,0:T(1,128)} %bitcast.2), custom_call_target="tpu_custom_call" | custom-call | tf_op jit(solution)/shard_map/distill/pallas_call | solution.py:474
  102.7 0.0 copy-start
  102.7 6.4 %grad.1 = f32[2048,1024]{1,0:T(8,128)} custom-call(bf16[2048,512]{1,0:T(8,128)(2,1)} %get-tuple-element.5.st_ref, bf16[512,1024]{1,0:T(8,128)(2,1)} %get-tuple-element.6.dz_ref), custom_call_target="tpu_custom_call" | custom-call | tf_op jit(solution)/shard_map/grad/pallas_call | solution.py:447
  109.2 0.0 copy-done
  109.2 0.5 copy.8
Async XLA Ops:
  102.7 6.5 %copy-start = (f32[1,128]{1,0:T(1,128)S(1)}, f32[1,128]{1,0:T(1,128)}, u32[]{:S(2)}) copy-start(f32[1,128]{1,0:T(1,128)} %get-tuple-element.7) | copy-start | bytes 1540

commit v7 on v6

--- a/solution.py
+++ b/solution.py
@@ -94,27 +94,23 @@
     def wait_piece(t, s, c):
         pltpu.make_async_copy(xbuf.at[t, s, c], xbuf.at[t, s, c], x_recv.at[t, s, c]).wait()
 
-    def own(t):
-        copy_a(t, 0).start()
-
-        @pl.when(mid)
+    def start_on(middle, *copies):
+        @pl.when(mid if middle else jnp.logical_not(mid))
         def _():
-            copy_b(t, 0).start()
-
-    def event(t, i):
-        wait_piece(t, order[i], x)
-
-        @pl.when(mid)
+            for c in copies:
+                c.start()
+
+    def event(t, i, middle):
+        @pl.when(mid if middle else jnp.logical_not(mid))
         def _():
-            (copy_b(t, 1) if i == 1 else copy_a(t, i)).start()
-
-        if not (t == 2 and i == 1):
-            copy_x(t, i).start()
+            wait_piece(t, order[i], x)
+            if middle:
+                (copy_b(t, 1) if i == 1 else copy_a(t, i)).start()
+            if not (t == 2 and i == 1):
+                copy_x(t, i).start()
 
     def other(t, i):
         wait_piece(t, order[i], ox)
-        if t == 2 and i == 0:
-            copy_a(t, 1).start()
 
     def dot_block(t, b, cs):
         return jnp.dot(xbuf[t, b].reshape(block, width), wbuf[t, :, cs], preferred_element_type=F32)
@@ -260,52 +256,69 @@
         arrived(tall.at[across, b], g_recv.at[across, b])
         g_copy(i, 2).start()
 
-    own(0)
-    copy_x(0, 0).start()
-    copy_x(1, 0).start()
+    for t in range(2):
+        copy_a(t, 0).start()
+        start_on(True, copy_b(t, 0))
+        copy_x(t, 0).start()
     for c in o_copies:
         c.start()
-    own(1)
-    copy_x(2, 0).start()
-    event(0, 1)
+    event(0, 1, True)
+    event(1, 1, True)
+    event(0, 2, True)
+    event(1, 2, True)
+    start_on(True, copy_b(2, 0), copy_x(2, 0))
+    event(0, 1, False)
     x_copies[0].wait()
     w_copies[0].wait()
     other(0, 0)
     student(0)
-    event(0, 2)
-    event(1, 1)
-    event(0, 3)
+    event(1, 1, False)
+    start_on(False, copy_a(2, 0))
     x_copies[1].wait()
     w_copies[1].wait()
+    event(0, 3, True)
     other(1, 0)
     teacher_first(0)
+    event(0, 2, False)
+    event(1, 3, True)
+    start_on(True, copy_a(2, 0))
     other(0, 1)
     student(1)
-    event(1, 2)
-    own(2)
+    event(1, 2, False)
+    start_on(False, copy_x(2, 0))
+    event(2, 1, True)
+    other(1, 1)
+    teacher_first(1)
+    event(0, 3, False)
+    event(2, 2, True)
     other(0, 2)
     student(2)
-    event(1, 3)
-    other(0, 3)
-    student(3)
-    event(2, 1)
-    other(2, 0)
-    other(1, 1)
-    teacher_first(1)
-    event(2, 2)
-    student_sum()
+    event(1, 3, False)
     other(1, 2)
     teacher_first(2)
+    event(2, 3, True)
     x_copies[2].wait()
     w_copies[2].wait()
     for d in range(1, groups):
         o = other_mp(d)
         arrived(obuf.at[o], o_recv.at[o])
+    other(2, 0)
+    copy_a(2, 1).start()
     teacher_second(0)
-    event(2, 3)
-    student_relay()
+    event(2, 2, False)
+    other(0, 3)
+    student(3)
+    event(2, 3, False)
     other(1, 3)
     teacher_first(3)
+    student_sum()
+    transpose(0)
+    transpose(1)
+
+    @pl.when(jnp.logical_not(mid))
+    def _():
+        wait_piece(2, order[1], x)
+
     other(2, 1)
     teacher_second(1)
     target_sum(0)
@@ -313,12 +326,11 @@
     teacher_second(2)
     target_sum(1)
     target_relay(0)
+    student_relay()
     other(2, 3)
     teacher_second(3)
     target_sum(2)
     target_relay(1)
-    transpose(0)
-    transpose(1)
     target_sum(3)
 
     statr[dp] = stm[...].T[0:8, :]

time: 110 us -> 106 us (0.964)
  Pallas kernels: 109 us -> 104 us
    pallas_call x1, Pallas kernels: 102 us -> 98 us  [fused_shards(): pl.pallas_call(functools.partial(kernel, total_rows), out_shape=(jax.Shap...]
where the time goes in v7:
time: 106 us
  Pallas kernels  104 us (98%)
    pallas_call x1, Pallas kernels, fused_shards(): pl.pallas_call(functools.partial(kernel, total_rows), out_shape=(jax.Shap...  98 us
    pallas_call x1, Pallas kernels, grad_matmul(): pl.pallas_call(grad_kernel, in_specs=[any_spec, any_spec], out_specs=any_...  6.44 us

profile of v7, /device:TPU:0, one launch (start us, length us, event | category | flops | bytes accessed | tf_op | source)
XLA Modules:
  0.0 105.6 jit_solution(4782511505227356862)
XLA Ops:
  0.6 98.0 %distill.1 = (f32[1,128]{1,0:T(1,128)}, bf16[512,1024]{1,0:T(8,128)(2,1)}, bf16[2048,512]{1,0:T(8,128)(2,1)}) custom-call(bf16[64,4096]{1,0:T(8,128)(2,1)} %teacher_ref.1, bf16[4096,1024]{1,0:T(8,128)(2,1)} %weight_ref.1, bf16[64,2048]{1,0:T(8,128)(2,1)} %student_ref.1, bf16[2048,1024]{1,0:T(8,128)(2,1)} %projection_ref.1, s32[1,128]{1,0:T(1,128)} %bitcast.2), custom_call_target="tpu_custom_call" | custom-call | tf_op jit(solution)/shard_map/distill/pallas_call | solution.py:486
  98.7 0.0 copy-start
  98.7 6.4 %grad.1 = f32[2048,1024]{1,0:T(8,128)} custom-call(bf16[2048,512]{1,0:T(8,128)(2,1)} %get-tuple-element.5.st_ref, bf16[512,1024]{1,0:T(8,128)(2,1)} %get-tuple-element.6.dz_ref), custom_call_target="tpu_custom_call" | custom-call | tf_op jit(solution)/shard_map/grad/pallas_call | solution.py:459
  105.1 0.0 copy-done
  105.1 0.5 copy.8
Async XLA Ops:
  98.7 6.5 %copy-start = (f32[1,128]{1,0:T(1,128)S(1)}, f32[1,128]{1,0:T(1,128)}, u32[]{:S(2)}) copy-start(f32[1,128]{1,0:T(1,128)} %get-tuple-element.7) | copy-start | bytes 1540
